TPU v7x, 512 devices: a whole 4x8x8 slice. The times are simulated.
512 devices in a mesh: exp: 64 (over y, x, core), rep: 8 (over z).
Axes of the slice: x: 4, y: 8, z: 8, core: 2. Of those that a mesh axis runs over, the one named last changes fastest.
Arguments:
- tokens: bfloat16 [8192, 8192], P('exp', 'rep'), may hold values from -6 to 6
- down_weight: bfloat16 [8192, 2048], P('rep', 'exp'), may hold values from -0.0625 to 0.0625
- gate_proj: bfloat16 [64, 2048, 2048], P('exp', None, 'rep'), may hold values from -0.125 to 0.125
- up_proj: bfloat16 [64, 2048, 2048], P('exp', None, 'rep'), may hold values from -0.125 to 0.125
- out_proj: bfloat16 [64, 2048, 2048], P('exp', 'rep'), may hold values from -0.125 to 0.125
- up_weight: bfloat16 [2048, 8192], P('exp', 'rep'), may hold values from -0.125 to 0.125
- expert_ids: int32 [8192, 4], P('exp'), may hold values from 0 to 63, all different within a row; in each aligned block of 128 rows (0 to 127, 128 to 255, ...) at most 12 rows name the same one
- route_gates: float32 [8192, 4], P('exp'), may hold values from 0.1 to 1
Outputs:
- mixed: bfloat16 [8192, 8192], P('exp', 'rep')
Inputs may be any that keep to these rules, and one draw needn't show every extreme that they name: `expert_ids`: in each aligned block of 128 rows (the tokens of one index of exp), no expert is named by more than 12 rows, a bound that some block reaches.
All inputs are finite; a program needn't handle non-finite values.
Results may differ from a plain program's by a relative error of at most 0.035.
Values may be sent and summed in bfloat16 or wider, within the bound.
No kernel may reach another device: no remote copies, remote signals or barrier semaphores. Data moves between devices by JAX's collectives and lax.ppermute only.
A program may use at most 64 MiB of HBM per device.

v0:
```python
import jax
import jax.numpy as jnp
from jax import lax
from jax.sharding import PartitionSpec as P


def slot_targets(flat_ids, capacity):
    position = jnp.arange(flat_ids.shape[0], dtype=jnp.int32)
    same_id = flat_ids[:, None] == flat_ids[None, :]
    earlier = position[:, None] > position[None, :]
    slot_index = jnp.sum((same_id & earlier).astype(jnp.int32), axis=1)
    return flat_ids * capacity + slot_index


def on_device(
    tokens, down_weight, gate_proj, up_proj, out_proj, up_weight, expert_ids, route_gates
):
    tok_rows = tokens.shape[0]
    topk_count = expert_ids.shape[1]
    experts = lax.axis_size("exp")
    capacity = max(2, 3 * tok_rows * topk_count // (2 * experts))
    partial_latent = jnp.dot(
        tokens,
        lax.all_gather(down_weight, "exp", axis=1, tiled=True),
        preferred_element_type=jnp.float32,
    )
    flat_ids = expert_ids.reshape(-1)
    targets = slot_targets(flat_ids, capacity)
    owner_row = jnp.arange(flat_ids.shape[0], dtype=jnp.int32) // topk_count
    source_row = jnp.zeros((experts * capacity,), jnp.int32).at[targets].set(owner_row)
    filled = (
        jnp.zeros((experts * capacity,), jnp.bfloat16)
        .at[targets]
        .set(jnp.ones(flat_ids.shape, jnp.bfloat16))
    )
    latent_share = lax.psum_scatter(
        partial_latent.astype(jnp.bfloat16), "rep", scatter_dimension=1, tiled=True
    )
    full_rows = lax.all_gather(
        lax.all_to_all(
            (latent_share[source_row] * filled[:, None]).reshape(
                experts, capacity, latent_share.shape[1]
            ),
            "exp",
            split_axis=0,
            concat_axis=0,
            tiled=True,
        ),
        "rep",
        axis=2,
        tiled=True,
    )
    sources, slots, width = full_rows.shape
    flat_rows = full_rows.reshape(sources * slots, width)
    gate_act = jnp.dot(flat_rows, gate_proj[0], preferred_element_type=jnp.float32)
    up_act = jnp.dot(flat_rows, up_proj[0], preferred_element_type=jnp.float32)
    hidden = (jax.nn.silu(gate_act) * up_act).astype(jnp.bfloat16)
    partial_out = jnp.dot(hidden, out_proj[0], preferred_element_type=jnp.float32)
    partial_out = partial_out.reshape(sources, slots, width)
    finished = lax.psum_scatter(
        partial_out.astype(jnp.bfloat16), "rep", scatter_dimension=2, tiled=True
    ).astype(jnp.float32)
    returned = lax.all_to_all(
        finished.astype(jnp.bfloat16), "exp", split_axis=0, concat_axis=0, tiled=True
    ).astype(finished.dtype)
    slice_width = returned.shape[2]
    picked = returned.reshape(experts * capacity, slice_width)[targets]
    picked = picked.reshape(tok_rows, topk_count, slice_width)
    combined = jnp.sum(picked * route_gates[:, :, None], axis=1).astype(jnp.bfloat16)
    full_latent = lax.all_gather(combined, "rep", axis=1, tiled=True)
    mixed = jnp.dot(
        full_latent,
        lax.all_gather(up_weight, "exp", axis=0, tiled=True),
        preferred_element_type=jnp.float32,
    )
    return mixed.astype(jnp.bfloat16)


def solution(mesh):
    in_specs = (
        P("exp", "rep"),
        P("rep", "exp"),
        P("exp", None, "rep"),
        P("exp", None, "rep"),
        P("exp", "rep", None),
        P("exp", "rep"),
        P("exp", None),
        P("exp", None),
    )
    out_specs = P("exp", "rep")
    return jax.shard_map(
        on_device, mesh=mesh, in_specs=in_specs, out_specs=out_specs, check_vma=False
    )
```

profile of v0, /device:TPU:1, one launch (start us, length us, event | category | flops | bytes accessed | tf_op | source)
XLA Modules:
  0.0 393.1 jit_solution(9919942706435198406)
XLA Ops:
  6.5 0.7 all-gather.4.cloned.1.call-update
  7.3 93.7 %all-gather.4.cloned.1.call-done = bf16[1024,2048]{0,1:T(8,128)(2,1)} async-done(((bf16[1024,32]{0,1:T(8,128)(2,1)}), bf16[1024,2048]{0,1:T(8,128)(2,1)}) %all-gather.4.cloned.1.call-update) | async-done | bytes 4194320 | tf_op jit(solution)/shard_map/all_gather | solution.py:24
  101.0 4.6 %convolution_convert_fusion.1 = bf16[128,2048]{1,0:T(8,128)(2,1)} fusion(bf16[128,1024]{1,0:T(8,128)(2,1)} %param.8, bf16[1024,2048]{0,1:T(8,128)(2,1)} %all-gather.4.cloned.1.call-done), kind=kOutput, calls=%fused_computation.5 | convolution fusion | flops 537133056 | bytes 4980736 | tf_op jit(solution)/shard_map/dot_general | solution.py:22
  106.1 0.3 convert_reduce_fusion
  106.4 3.8 scatter_custom_fusion.1
  110.3 2.4 scatter_custom_fusion
  112.8 26.0 %reduce-scatter.3.cloned.1.call-done = bf16[128,256]{1,0:T(8,128)(2,1)} async-done(((bf16[128,2048]{1,0:T(8,128)(2,1)}), bf16[128,256]{1,0:T(8,128)(2,1)}) %reduce-scatter.3.cloned.1.call-update) | async-done | bytes 65552 | tf_op jit(solution)/shard_map/reduce_scatter | solution.py:36
  138.8 2.9 gather_fusion
  142.1 32.8 %all_to_all.10 = bf16[64,12,256]{2,1,0:T(8,128)(2,1)} all-to-all(bf16[64,12,256]{2,1,0:T(8,128)(2,1)S(1)} %broadcast_multiply_fusion), channel_id=1, replica_groups=mesh['exp'=64,'rep'=8] {'exp'}, dimensions={0} | all-to-all | bytes 786432 | tf_op jit(solution)/shard_map/all_to_all | solution.py:40
  175.0 56.9 %all-gather.6.cloned.1.call-done = bf16[64,12,2048]{2,1,0:T(8,128)(2,1)} async-done(((bf16[64,12,256]{2,1,0:T(8,128)(2,1)}), bf16[64,12,2048]{2,1,0:T(8,128)(2,1)}) %all-gather.6.cloned.1.call-update) | async-done | bytes 3145744 | tf_op jit(solution)/shard_map/all_gather | solution.py:39
  231.9 6.2 %reshape.54 = bf16[768,2048]{1,0:T(8,128)(2,1)} reshape(bf16[64,12,2048]{2,1,0:T(8,128)(2,1)} %all-gather.6.cloned.1.call-done) | data formatting | bytes 6291456 | tf_op jit(solution)/shard_map/reshape | solution.py:54
  238.1 3.0 fusion.3
  241.2 1.0 fusion
  242.3 2.7 convolution_convert_fusion
  245.0 0.5 all-gather.8.cloned.1.call-update
  245.6 47.6 %reduce-scatter.5.cloned.1.call-done = bf16[64,12,256]{2,0,1:T(8,128)(2,1)} async-done(((bf16[64,12,2048]{2,0,1:T(8,128)(2,1)}), bf16[64,12,256]{2,0,1:T(8,128)(2,1)}) %reduce-scatter.5.cloned.1.call-update) | async-done | bytes 393232 | tf_op jit(solution)/shard_map/reduce_scatter | solution.py:60
  293.2 2.0 copy.24
  295.2 12.9 %all-to-all-start.1 = ((bf16[64,12,256]{2,1,0:T(8,128)(2,1)}), bf16[64,12,256]{2,1,0:T(8,128)(2,1)S(1)}, u32[]{:S(2)}, u32[]{:S(2)}) async-start(bf16[64,12,256]{2,1,0:T(8,128)(2,1)} %copy.24), calls=%async_computation.3 | async-start | bytes 1048576 | tf_op jit(solution)/shard_map/all_to_all | solution.py:63
  308.2 18.4 %all-to-all-done.1 = bf16[64,12,256]{2,1,0:T(8,128)(2,1)S(1)} async-done(((bf16[64,12,256]{2,1,0:T(8,128)(2,1)}), bf16[64,12,256]{2,1,0:T(8,128)(2,1)S(1)}, u32[]{:S(2)}, u32[]{:S(2)}) %all-to-all-start.1) | async-done | bytes 393248 | tf_op jit(solution)/shard_map/all_to_all | solution.py:63
  326.7 1.6 gather_fusion.1
  328.4 0.4 multiply_reduce_fusion
  328.9 19.8 %all_gather.14 = bf16[128,2048]{1,0:T(8,128)(2,1)S(1)} all-gather(bf16[128,256]{1,0:T(8,128)(2,1)S(1)} %multiply_reduce_fusion), channel_id=1, replica_groups=mesh['exp'=64,'rep'=8] {'rep'}, dimensions={1}, use_global_device_ids=true | all-gather | bytes 589824 | tf_op jit(solution)/shard_map/all_gather | solution.py:70
  348.7 34.3 %all-gather.8.cloned.1.call-done = bf16[2048,1024]{1,0:T(8,128)(2,1)} async-done(((bf16[32,1024]{1,0:T(8,128)(2,1)}), bf16[2048,1024]{1,0:T(8,128)(2,1)}) %all-gather.8.cloned.1.call-update) | async-done | bytes 4194320 | tf_op jit(solution)/shard_map/all_gather | solution.py:73
  383.0 3.6 convolution_convert_fusion.2
  (38 shorter events, 1.6 us)
Async XLA Ops:
  6.5 235.7 %copy-start = (bf16[1,256,2048]{2,1,0:T(8,128)(2,1)S(1)}, bf16[1,256,2048]{2,1,0:T(8,128)(2,1)}, u32[]{:S(2)}) copy-start(bf16[1,256,2048]{2,1,0:T(8,128)(2,1)} %param.12) | copy-start | bytes 3145732
  6.5 99.1 %copy-start.2 = (s32[128,4]{0,1:T(4,128)S(1)}, s32[128,4]{0,1:T(4,128)}, u32[]{:S(2)}) copy-start(s32[128,4]{0,1:T(4,128)} %param.14) | copy-start | bytes 6148
  6.5 94.5 %all-gather.4.cloned.1.call-start = ((), (), s32[]{:S(2)}) async-start(), calls=%async_computation.4 | async-start | bytes 4259840 | tf_op jit(solution)/shard_map/all_gather | solution.py:24
  7.3 131.6 %reduce-scatter.3.cloned.1.call-start = ((), (), s32[]{:S(2)}) async-start(), calls=%async_computation.5 | async-start | bytes 589824 | tf_op jit(solution)/shard_map/reduce_scatter | solution.py:36
  105.6 126.3 %all-gather.6.cloned.1.call-start = ((), (), s32[]{:S(2)}) async-start(), calls=%async_computation.6 | async-start | bytes 4718592 | tf_op jit(solution)/shard_map/all_gather | solution.py:39
  174.9 63.2 %copy-start.4 = (bf16[1,2048,256]{2,1,0:T(8,128)(2,1)S(1)}, bf16[1,2048,256]{2,1,0:T(8,128)(2,1)}, u32[]{:S(2)}) copy-start(bf16[1,2048,256]{2,1,0:T(8,128)(2,1)} %param.10) | copy-start | bytes 3145732
  174.9 118.3 %reduce-scatter.5.cloned.1.call-start = ((), (), s32[]{:S(2)}) async-start(), calls=%async_computation.7 | async-start | bytes 3538944 | tf_op jit(solution)/shard_map/reduce_scatter | solution.py:60
  238.1 3.0 copy-start.1
  238.1 3.1 copy-start.5
  242.3 65.8 %copy-start.3 = (f32[128,4]{0,1:T(4,128)S(1)}, f32[128,4]{0,1:T(4,128)}, u32[]{:S(2)}) copy-start(f32[128,4]{0,1:T(4,128)} %param.15) | copy-start | bytes 6148
  245.0 138.0 %all-gather.8.cloned.1.call-start = ((), (), s32[]{:S(2)}) async-start(), calls=%async_computation.8 | async-start | bytes 4259840 | tf_op jit(solution)/shard_map/all_gather | solution.py:73
  295.2 31.4 %all-to-all-start.1 = ((bf16[64,12,256]{2,1,0:T(8,128)(2,1)}), bf16[64,12,256]{2,1,0:T(8,128)(2,1)S(1)}, u32[]{:S(2)}, u32[]{:S(2)}) async-start(bf16[64,12,256]{2,1,0:T(8,128)(2,1)} %copy.24), calls=%async_computation.3 | async-start | bytes 1048576 | tf_op jit(solution)/shard_map/all_to_all | solution.py:63
Sparse Core Ops, SparseCore 0:
  10.7 90.2 all-gather.3
  105.7 33.0 reduce-scatter.2
  175.0 56.8 all-gather.5
  245.1 48.0 reduce-scatter.4
  296.9 86.0 all-gather.7
where the time goes:
time: 394 us; the launch traced here: 393 us
  waiting for transfers between devices  278 us (71%)
  blocking collectives  52.7 us (13%)
  local copies, waits for them, and re-layouts  20.1 us (5%)
  matrix products  14.9 us (4%)
  between operations  13.3 us (3%)
  starting transfers between devices  13 us (3%)
    all_gather x1, waiting for transfers between devices, on_device(): lax.all_gather(down_weight, 'exp', axis=1, tiled=True)  93.7 us
    all_gather x1, waiting for transfers between devices, on_device(): lax.all_gather(lax.all_to_all((latent_share[source_row] * filled[:, None]...  56.9 us
    reduce_scatter x1, waiting for transfers between devices, on_device(): lax.psum_scatter(partial_out.astype(jnp.bfloat16), 'rep', scatter_dimensi...  47.6 us
    all_gather x1, waiting for transfers between devices, on_device(): lax.all_gather(up_weight, 'exp', axis=0, tiled=True)  34.3 us
    all_to_all x1, blocking collectives, on_device(): lax.all_to_all((latent_share[source_row] * filled[:, None]).reshape(exper...  32.8 us
    reduce_scatter x1, waiting for transfers between devices, on_device(): lax.psum_scatter(partial_latent.astype(jnp.bfloat16), 'rep', scatter_dime...  26 us
    all_gather x1, blocking collectives, on_device(): full_latent = lax.all_gather(combined, 'rep', axis=1, tiled=True)  19.8 us
    all_to_all x1, waiting for transfers between devices, on_device(): lax.all_to_all(finished.astype(jnp.bfloat16), 'exp', split_axis=0, concat...  18.4 us
  transfers between devices with their start and end apart: 6, of which 6 were waited for; matrix products, arithmetic and copies ran while one was open for 3% of the time, Pallas kernels for 0%

commit v1 on v0

v1 whole, which is shorter than its diff:
```python
import jax
import jax.numpy as jnp
from jax import lax
from jax.sharding import Mesh, PartitionSpec as P


def spread(x, axis):
    copies = jnp.broadcast_to(x[None], (lax.axis_size(axis),) + x.shape)
    return lax.all_to_all(copies, axis, split_axis=0, concat_axis=0, tiled=True)


def expert_counts(ids_t, experts):
    tok = ids_t.shape[1]
    expert = lax.broadcasted_iota(jnp.int32, (experts, tok), 0)
    one_hot = jnp.zeros((experts, tok), jnp.bool_)
    for k in range(ids_t.shape[0]):
        one_hot = one_hot | (ids_t[k][None, :] == expert)
    earlier = lax.broadcasted_iota(jnp.int32, (tok, tok), 0) < lax.broadcasted_iota(
        jnp.int32, (tok, tok), 1
    )
    counts = jnp.dot(
        one_hot.astype(jnp.bfloat16),
        earlier.astype(jnp.bfloat16),
        preferred_element_type=jnp.float32,
    ).astype(jnp.int32)
    return one_hot, counts


def on_device(
    tokens, down_weight, gate_proj, up_proj, out_proj, up_weight, expert_ids, route_gates
):
    tok_rows = tokens.shape[0]
    topk_count = expert_ids.shape[1]
    ny, nk, nr = lax.axis_size("y"), lax.axis_size("k"), lax.axis_size("rep")
    experts = ny * nk
    capacity = max(2, 3 * tok_rows * topk_count // (2 * experts))
    width = gate_proj.shape[1]
    unit = down_weight.shape[1]
    slice_width = width // nr

    swap = [(i * nr + j, j * nr + i) for i in range(nk) for j in range(nr)]
    ids_t = expert_ids.T
    sent_ids_t = lax.ppermute(ids_t, ("k", "rep"), swap)

    all_tokens = lax.all_gather(tokens, "k", axis=0, tiled=True)
    down_cols = spread(down_weight.T, "y").reshape(ny * unit, down_weight.shape[0])
    one_hot, counts = expert_counts(sent_ids_t, experts)
    slot = lax.broadcasted_iota(jnp.int32, (experts, capacity, tok_rows), 1)
    select = ((counts[:, None, :] == slot) & one_hot[:, None, :]).astype(jnp.bfloat16)
    _, own_counts = expert_counts(ids_t, experts)
    own_slot = jnp.take_along_axis(own_counts, ids_t, axis=0)
    targets = (ids_t * capacity + own_slot).T.reshape(-1)

    partial_latent = lax.dot_general(
        all_tokens, down_cols, (((1,), (1,)), ((), ())), preferred_element_type=jnp.float32
    )
    pieces = lax.all_to_all(
        partial_latent.astype(jnp.bfloat16).reshape(nr, tok_rows, ny * unit),
        "rep", split_axis=0, concat_axis=0, tiled=True,
    )
    latent = jnp.sum(pieces.astype(jnp.float32), axis=0).astype(jnp.bfloat16)
    send = lax.dot_general(
        select, latent, (((2,), (0,)), ((), ())), preferred_element_type=jnp.float32
    ).astype(jnp.bfloat16)
    got = lax.all_to_all(send, ("y", "k"), split_axis=0, concat_axis=0, tiled=True)
    rows = got.reshape(ny, nk, capacity, ny * unit).transpose(0, 2, 1, 3)
    rows = rows.reshape(ny * capacity, width)
    rows, up_weight = lax.optimization_barrier((rows, up_weight))
    full_rows = lax.all_gather(rows, "rep", axis=0, tiled=True)
    up_rows = spread(up_weight, "y")

    def reorder(w):
        return w.reshape(ny, nk, unit, w.shape[1]).transpose(1, 0, 2, 3).reshape(w.shape)

    gate_act = jnp.dot(full_rows, reorder(gate_proj[0]), preferred_element_type=jnp.float32)
    up_act = jnp.dot(full_rows, reorder(up_proj[0]), preferred_element_type=jnp.float32)
    hidden = (jax.nn.silu(gate_act) * up_act).astype(jnp.bfloat16)
    partial_out = jnp.dot(
        hidden, out_proj[0], preferred_element_type=jnp.float32
    ).astype(jnp.bfloat16)
    finished = lax.psum_scatter(partial_out, "rep", scatter_dimension=1, tiled=True)
    finished, up_rows = lax.optimization_barrier((finished, up_rows))
    all_up = lax.all_gather(up_rows, "k", axis=0, tiled=False)
    back = finished.reshape(nr, ny, capacity, slice_width).transpose(1, 0, 2, 3)
    returned = lax.all_to_all(
        back.reshape(experts, capacity, slice_width),
        ("y", "k"), split_axis=0, concat_axis=0, tiled=True,
    )
    picked = returned.astype(jnp.float32).reshape(experts * capacity, slice_width)[targets]
    picked = picked.reshape(tok_rows, topk_count, slice_width)
    combined = jnp.sum(picked * route_gates[:, :, None], axis=1).astype(jnp.bfloat16)
    full_latent = spread(combined, "rep").transpose(1, 0, 2).reshape(tok_rows, width)
    all_up = all_up.transpose(1, 0, 2, 3).reshape(width, up_weight.shape[1])
    mixed = jnp.dot(full_latent, all_up, preferred_element_type=jnp.float32)
    return mixed.astype(jnp.bfloat16)


def solution(mesh):
    nexp, nrep = mesh.devices.shape
    fine = Mesh(mesh.devices.reshape(nexp // nrep, nrep, nrep), ("y", "k", "rep"))
    exp = ("y", "k")
    in_specs = (
        P(exp, "rep"),
        P("rep", exp),
        P(exp, None, "rep"),
        P(exp, None, "rep"),
        P(exp, "rep", None),
        P(exp, "rep"),
        P(exp, None),
        P(exp, None),
    )
    return jax.shard_map(
        on_device, mesh=fine, in_specs=in_specs, out_specs=P(exp, "rep"), check_vma=False
    )
```

time: 394 us -> 269 us (0.68)
  waiting for transfers between devices: 278 us -> 118 us
  blocking collectives: 52.7 us -> 72.6 us
  starting transfers between devices: 13 us -> 28.8 us
    all_gather x3, waiting for transfers between devices: 185 us -> 58.7 us  [the longest x1 38.5 us: on_device(): full_rows = lax.all_gather(rows, 'rep', axis=0, tiled=True)]
    reduce_scatter x2 -> x1, waiting for transfers between devices: 73.6 us -> 22.5 us  [on_device(): lax.psum_scatter(partial_out, 'rep', scatter_dimension=1, tiled=True)]
    all_to_all x1 -> x3, blocking collectives: 32.8 us -> 72.6 us  [the longest x2 44.5 us: spread(): return lax.all_to_all(copies, axis, split_axis=0, concat_axis=0, tiled=True)]
    all_gather x1 -> x0, blocking collectives: 19.8 us -> none  [on_device(): full_latent = lax.all_gather(combined, 'rep', axis=1, tiled=True)]
    all_to_all x1 -> x3, starting transfers between devices: 12.9 us -> 24.7 us  [the longest x1 12.8 us: on_device(): lax.all_to_all(back.reshape(experts, capacity, slice_width), ('y', 'k'),...]
    ppermute x0 -> x1, waiting for transfers between devices: none -> 9.83 us  [on_device(): sent_ids_t = lax.ppermute(ids_t, ('k', 'rep'), swap)]
    all_to_all x1 -> x3, waiting for transfers between devices: 18.4 us -> 25.9 us  [the longest x1 13.7 us: on_device(): lax.all_to_all(back.reshape(experts, capacity, slice_width), ('y', 'k'),...]
    transpose x0 -> x4, local copies, waits for them, and re-layouts: none -> 6.38 us  [the longest x1 4.98 us: on_device(): all_up = all_up.transpose(1, 0, 2, 3).reshape(width, up_weight.shape[1])]
  transfers between devices with their start and end apart: 6 -> 8, of which waited for: 6 -> 8; matrix products, arithmetic and copies ran while one was open for 3% -> 6% of each run, Pallas kernels for 0% -> 0%
where the time goes in v1:
time: 269 us
  waiting for transfers between devices  118 us (44%)
  blocking collectives  72.6 us (27%)
  starting transfers between devices  28.8 us (11%)
  local copies, waits for them, and re-layouts  18.3 us (7%)
  matrix products  17.4 us (6%)
  between operations  13.3 us (5%)
    all_to_all x2, blocking collectives, spread(): return lax.all_to_all(copies, axis, split_axis=0, concat_axis=0, tiled=True)  44.5 us
    all_gather x1, waiting for transfers between devices, on_device(): full_rows = lax.all_gather(rows, 'rep', axis=0, tiled=True)  38.5 us
    all_to_all x1, blocking collectives, on_device(): lax.all_to_all(send, ('y', 'k'), split_axis=0, concat_axis=0, tiled=True)  28 us
    reduce_scatter x1, waiting for transfers between devices, on_device(): lax.psum_scatter(partial_out, 'rep', scatter_dimension=1, tiled=True)  22.5 us
    all_gather x1, waiting for transfers between devices, on_device(): all_tokens = lax.all_gather(tokens, 'k', axis=0, tiled=True)  15.6 us
    all_to_all x1, waiting for transfers between devices, on_device(): lax.all_to_all(back.reshape(experts, capacity, slice_width), ('y', 'k'),...  13.7 us
    all_to_all x1, starting transfers between devices, on_device(): lax.all_to_all(back.reshape(experts, capacity, slice_width), ('y', 'k'),...  12.8 us
    ppermute x1, waiting for transfers between devices, on_device(): sent_ids_t = lax.ppermute(ids_t, ('k', 'rep'), swap)  9.83 us
  transfers between devices with their start and end apart: 8, of which 8 were waited for; matrix products, arithmetic and copies ran while one was open for 6% of the time, Pallas kernels for 0%

profile of v1, /device:TPU:1, one launch (start us, length us, event | category | flops | bytes accessed | tf_op | source)
XLA Modules:
  0.0 268.7 jit_solution(12775599507531999105)
XLA Ops:
  8.2 22.2 %all_to_all.30 = bf16[8,32,1024]{2,1,0:T(8,128)(2,1)S(1)} all-to-all(bf16[8,32,1024]{2,1,0:T(8,128)(2,1)S(1)} %broadcast_in_dim.10), channel_id=1, replica_groups=mesh['y'=8,'k'=8,'rep'=8] {'y'}, dimensions={0} | all-to-all | bytes 1048576 | tf_op jit(solution)/shard_map/all_to_all | solution.py:9
  30.4 15.6 %all-gather.5.cloned.1.call-done = bf16[1024,1024]{1,0:T(8,128)(2,1)} async-done(((bf16[128,1024]{1,0:T(8,128)(2,1)}), bf16[1024,1024]{1,0:T(8,128)(2,1)}) %all-gather.5.cloned.1.call-update) | async-done | bytes 2097168 | tf_op jit(solution)/shard_map/all_gather | solution.py:45
  45.9 3.2 %convolution_convert_fusion.1 = bf16[1024,256]{1,0:T(8,128)(2,1)} fusion(bf16[1024,1024]{1,0:T(8,128)(2,1)} %all-gather.5.cloned.1.call-done, bf16[256,1024]{1,0:T(8,128)(2,1)S(1)} %bitcast.86), kind=kOutput, calls=%fused_computation.3 | convolution fusion | flops 537133056 | bytes 3145728 | tf_op jit(solution)/shard_map/dot_general | solution.py:54
  49.1 7.2 %all-to-all-start.1 = ((bf16[8,128,256]{2,1,0:T(8,128)(2,1)}), bf16[8,128,256]{2,1,0:T(8,128)(2,1)S(1)}, u32[]{:S(2)}, u32[]{:S(2)}) async-start(bf16[8,128,256]{2,1,0:T(8,128)(2,1)} %bitcast.7), calls=%async_computation.1 | async-start | bytes 1048576 | tf_op jit(solution)/shard_map/all_to_all | solution.py:57
  56.4 4.0 %collective-permute-start = (s32[4,128]{1,0:T(4,128)S(1)}, s32[4,128]{1,0:T(4,128)S(1)}, u32[]{:S(2)}, u32[]{:S(2)}) collective-permute-start(s32[4,128]{1,0:T(4,128)S(1)} %bitcast.88), channel_id=1, source_target_pairs={{0,0},{1,8},{2,16},{3,24},{4,32},{5,40},{6,48},{7,56},{8,1},{9,9},... | collective-permute-start | bytes 6152 | tf_op jit(solution)/shard_map/ppermute | solution.py:43
  60.4 9.8 %collective-permute-done = s32[4,128]{1,0:T(4,128)S(1)} collective-permute-done((s32[4,128]{1,0:T(4,128)S(1)}, s32[4,128]{1,0:T(4,128)S(1)}, u32[]{:S(2)}, u32[]{:S(2)}) %collective-permute-start) | collective-permute-done | bytes 2080 | tf_op jit(solution)/shard_map/ppermute | solution.py:43
  70.4 3.9 %all-to-all-done.1 = bf16[8,128,256]{2,1,0:T(8,128)(2,1)S(1)} async-done(((bf16[8,128,256]{2,1,0:T(8,128)(2,1)}), bf16[8,128,256]{2,1,0:T(8,128)(2,1)S(1)}, u32[]{:S(2)}, u32[]{:S(2)}) %all-to-all-start.1) | async-done | bytes 524320 | tf_op jit(solution)/shard_map/all_to_all | solution.py:57
  74.9 28.0 %all_to_all.31 = bf16[64,12,256]{2,1,0:T(8,128)(2,1)S(1)} all-to-all(bf16[64,12,256]{2,1,0:T(8,128)(2,1)S(1)} %copy.23), channel_id=1, replica_groups=mesh['y'=8,'k'=8,'rep'=8] {'y','k'}, dimensions={0} | all-to-all | bytes 786432 | tf_op jit(solution)/shard_map/all_to_all | solution.py:65
  104.0 1.1 copy.25
  105.2 38.5 %all-gather.7.cloned.1.call-done = bf16[768,2048]{1,0:T(8,128)(2,1)} async-done(((bf16[96,2048]{1,0:T(8,128)(2,1)}), bf16[768,2048]{1,0:T(8,128)(2,1)}) %all-gather.7.cloned.1.call-update) | async-done | bytes 3145744 | tf_op jit(solution)/shard_map/all_gather | solution.py:69
  143.6 3.1 %fusion.32 = f32[768,256]{1,0:T(8,128)S(1)} fusion(bf16[768,2048]{1,0:T(8,128)(2,1)} %all-gather.7.cloned.1.call-done, bf16[2048,256]{1,0:T(8,128)(2,1)} %bitcast.85), kind=kOutput, calls=%fused_computation.63 | convolution fusion | flops 805306368 | bytes 4980736 | tf_op jit(solution)/shard_map/dot_general | solution.py:75
  146.8 6.9 %convolution_convert_fusion = bf16[768,2048]{1,0:T(8,128)(2,1)} fusion(bf16[768,2048]{1,0:T(8,128)(2,1)} %all-gather.7.cloned.1.call-done, bf16[2048,256]{1,0:T(8,128)(2,1)S(1)} %bitcast.84, bf16[1,256,2048]{2,1,0:T(8,128)(2,1)S(1)} %copy-done, f32[768,256]{1,0:T(8,128)S(1)} %fusion.32), kind=kOutput, calls=%fused_computation.2 | convolution fusion | flops 1613365248 | bytes 9175040 | tf_op jit(solution)/shard_map/dot_general | solution.py:78
  154.6 22.4 %all_to_all.32 = bf16[8,32,1024]{2,1,0:T(8,128)(2,1)} all-to-all(bf16[8,32,1024]{2,1,0:T(8,128)(2,1)S(1)} %broadcast_in_dim.11), channel_id=1, replica_groups=mesh['y'=8,'k'=8,'rep'=8] {'y'}, dimensions={0} | all-to-all | bytes 1048576 | tf_op jit(solution)/shard_map/all_to_all | solution.py:9
  176.9 22.5 %reduce-scatter.2.cloned.1.call-done = bf16[768,256]{1,0:T(8,128)(2,1)} async-done(((bf16[768,2048]{1,0:T(8,128)(2,1)}), bf16[768,256]{1,0:T(8,128)(2,1)}) %reduce-scatter.2.cloned.1.call-update) | async-done | bytes 393232 | tf_op jit(solution)/shard_map/reduce_scatter | solution.py:81
  199.7 1.1 reshape.153
  202.0 12.8 %all-to-all-start.4 = ((bf16[64,12,256]{2,1,0:T(8,128)(2,1)}), bf16[64,12,256]{2,1,0:T(8,128)(2,1)S(1)}, u32[]{:S(2)}, u32[]{:S(2)}) async-start(bf16[64,12,256]{2,1,0:T(8,128)(2,1)} %copy.28), calls=%async_computation.5 | async-start | bytes 1048576 | tf_op jit(solution)/shard_map/all_to_all | solution.py:85
  214.8 3.7 %gather_fusion.1 = s32[512]{0:T(512)S(1)} fusion(s32[64,128]{1,0:T(8,128)S(1)} %convolution_convert_fusion.4, s32[512]{0:T(512)S(1)} %fusion.28), kind=kCustom, calls=%fused_computation.1 | custom fusion | bytes 8192 | tf_op jit(solution)/shard_map/jit(take_along_axis)/gather | solution.py:51
  219.0 13.7 %all-to-all-done.4 = bf16[64,12,256]{2,1,0:T(8,128)(2,1)S(1)} async-done(((bf16[64,12,256]{2,1,0:T(8,128)(2,1)}), bf16[64,12,256]{2,1,0:T(8,128)(2,1)S(1)}, u32[]{:S(2)}, u32[]{:S(2)}) %all-to-all-start.4) | async-done | bytes 393248 | tf_op jit(solution)/shard_map/all_to_all | solution.py:85
  232.7 1.6 gather_fusion
  235.9 4.7 %all-to-all-start.5 = ((bf16[8,128,256]{1,2,0:T(8,128)(2,1)}), bf16[8,128,256]{1,2,0:T(8,128)(2,1)S(1)}, u32[]{:S(2)}, u32[]{:S(2)}) async-start(bf16[8,128,256]{1,2,0:T(8,128)(2,1)} %broadcast_in_dim.13), calls=%async_computation.6 | async-start | bytes 1048576 | tf_op jit(solution)/shard_map/all_to_all | solution.py:9
  240.6 4.6 %all-gather.9.cloned.1.call-done = bf16[64,32,1024]{2,1,0:T(8,128)(2,1)} async-done(((bf16[8,32,1024]{2,1,0:T(8,128)(2,1)}), bf16[64,32,1024]{2,1,0:T(8,128)(2,1)}) %all-gather.9.cloned.1.call-update) | async-done | bytes 4194320 | tf_op jit(solution)/shard_map/all_gather | solution.py:83
  245.2 5.0 %copy.32 = bf16[8,8,32,1024]{3,2,1,0:T(8,128)(2,1)} copy(bf16[8,8,32,1024]{3,2,0,1:T(8,128)(2,1)} %bitcast.75) | data formatting | bytes 8388608 | tf_op jit(solution)/shard_map/transpose | solution.py:93
  250.2 8.4 %all-to-all-done.5 = bf16[8,128,256]{1,2,0:T(8,128)(2,1)S(1)} async-done(((bf16[8,128,256]{1,2,0:T(8,128)(2,1)}), bf16[8,128,256]{1,2,0:T(8,128)(2,1)S(1)}, u32[]{:S(2)}, u32[]{:S(2)}) %all-to-all-start.5) | async-done | bytes 524320 | tf_op jit(solution)/shard_map/all_to_all | solution.py:9
  258.5 3.6 %convolution_convert_fusion.3 = bf16[128,1024]{1,0:T(8,128)(2,1)} fusion(bf16[128,2048]{0,1:T(8,128)(2,1)S(1)} %bitcast.76, bf16[2048,1024]{1,0:T(8,128)(2,1)} %bitcast.74), kind=kOutput, calls=%fused_computation.7 | convolution fusion | flops 537001984 | bytes 4980736 | tf_op jit(solution)/shard_map/dot_general | solution.py:94
  (47 shorter events, 7.8 us)
Async XLA Ops:
  6.5 140.3 %copy-start = (bf16[1,256,2048]{2,1,0:T(8,128)(2,1)S(1)}, bf16[1,256,2048]{2,1,0:T(8,128)(2,1)}, u32[]{:S(2)}) copy-start(bf16[1,256,2048]{2,1,0:T(8,128)(2,1)} %param.12) | copy-start | bytes 3145732
  6.5 39.4 %all-gather.5.cloned.1.call-start = ((), (), s32[]{:S(2)}) async-start(), calls=%async_computation.7 | async-start | bytes 2359296 | tf_op jit(solution)/shard_map/all_gather | solution.py:45
  45.9 10.4 %copy-start.4 = (s32[128,4]{0,1:T(4,128)S(1)}, s32[128,4]{0,1:T(4,128)}, u32[]{:S(2)}) copy-start(s32[128,4]{0,1:T(4,128)} %param.14) | copy-start | bytes 6148
  49.1 54.9 %copy-start.1 = (bf16[1,2048,256]{2,1,0:T(8,128)(2,1)S(1)}, bf16[1,2048,256]{2,1,0:T(8,128)(2,1)}, u32[]{:S(2)}) copy-start(bf16[1,2048,256]{2,1,0:T(8,128)(2,1)} %param.10) | copy-start | bytes 3145732
  49.1 25.2 %all-to-all-start.1 = ((bf16[8,128,256]{2,1,0:T(8,128)(2,1)}), bf16[8,128,256]{2,1,0:T(8,128)(2,1)S(1)}, u32[]{:S(2)}, u32[]{:S(2)}) async-start(bf16[8,128,256]{2,1,0:T(8,128)(2,1)} %bitcast.7), calls=%async_computation.1 | async-start | bytes 1048576 | tf_op jit(solution)/shard_map/all_to_all | solution.py:57
  56.3 87.3 %all-gather.7.cloned.1.call-start = ((), (), s32[]{:S(2)}) async-start(), calls=%async_computation.8 | async-start | bytes 3538944 | tf_op jit(solution)/shard_map/all_gather | solution.py:69
  56.4 13.9 %collective-permute-start = (s32[4,128]{1,0:T(4,128)S(1)}, s32[4,128]{1,0:T(4,128)S(1)}, u32[]{:S(2)}, u32[]{:S(2)}) collective-permute-start(s32[4,128]{1,0:T(4,128)S(1)} %bitcast.88), channel_id=1, source_target_pairs={{0,0},{1,8},{2,16},{3,24},{4,32},{5,40},{6,48},{7,56},{8,1},{9,9},... | collective-permute-start | bytes 6152 | tf_op jit(solution)/shard_map/ppermute | solution.py:43
  74.6 30.4 %copy-start.2 = (bf16[1,2048,256]{2,1,0:T(8,128)(2,1)S(1)}, bf16[1,2048,256]{2,1,0:T(8,128)(2,1)}, u32[]{:S(2)}) copy-start(bf16[1,2048,256]{2,1,0:T(8,128)(2,1)} %param.11) | copy-start | bytes 3145732
  103.9 95.6 %reduce-scatter.2.cloned.1.call-start = ((), (), s32[]{:S(2)}) async-start(), calls=%async_computation.9 | async-start | bytes 3538944 | tf_op jit(solution)/shard_map/reduce_scatter | solution.py:81
  153.7 0.8 copy-start.3
  153.7 91.5 %all-gather.9.cloned.1.call-start = ((), (), s32[]{:S(2)}) async-start(), calls=%async_computation.10 | async-start | bytes 4718592 | tf_op jit(solution)/shard_map/all_gather | solution.py:83
  199.7 19.2 %copy-start.5 = (f32[128,4]{0,1:T(4,128)S(1)}, f32[128,4]{0,1:T(4,128)}, u32[]{:S(2)}) copy-start(f32[128,4]{0,1:T(4,128)} %param.15) | copy-start | bytes 6148
  202.0 30.6 %all-to-all-start.4 = ((bf16[64,12,256]{2,1,0:T(8,128)(2,1)}), bf16[64,12,256]{2,1,0:T(8,128)(2,1)S(1)}, u32[]{:S(2)}, u32[]{:S(2)}) async-start(bf16[64,12,256]{2,1,0:T(8,128)(2,1)} %copy.28), calls=%async_computation.5 | async-start | bytes 1048576 | tf_op jit(solution)/shard_map/all_to_all | solution.py:85
  235.9 22.6 %all-to-all-start.5 = ((bf16[8,128,256]{1,2,0:T(8,128)(2,1)}), bf16[8,128,256]{1,2,0:T(8,128)(2,1)S(1)}, u32[]{:S(2)}, u32[]{:S(2)}) async-start(bf16[8,128,256]{1,2,0:T(8,128)(2,1)} %broadcast_in_dim.13), calls=%async_computation.6 | async-start | bytes 1048576 | tf_op jit(solution)/shard_map/all_to_all | solution.py:9
Sparse Core Ops, SparseCore 0:
  9.5 36.3 all-gather.4
  104.0 39.5 all-gather.6
  153.8 45.5 reduce-scatter.1
  201.5 43.6 all-gather.8

commit v2 on v1

--- a/solution.py
+++ b/solution.py
@@ -1,6 +1,10 @@
+import functools
+
 import jax
 import jax.numpy as jnp
 from jax import lax
+from jax.experimental import pallas as pl
+from jax.experimental.pallas import tpu as pltpu
 from jax.sharding import Mesh, PartitionSpec as P
 
 
@@ -24,6 +28,107 @@
         preferred_element_type=jnp.float32,
     ).astype(jnp.int32)
     return one_hot, counts
+
+
+def expert_kernel(steps, per, x_ref, gate_ref, up_ref, out_ref, y_ref, gate_sum, up_sum, hidden):
+    step = pl.program_id(0)
+    depth = x_ref.shape[1] // per
+
+    @pl.when(step == 0)
+    def _():
+        gate_sum[...] = jnp.zeros_like(gate_sum)
+        up_sum[...] = jnp.zeros_like(up_sum)
+
+    @pl.when(step < steps)
+    def _():
+        for j in range(per):
+            x = x_ref[:, j * depth : (j + 1) * depth]
+            w = gate_ref[:, j].reshape(depth, gate_ref.shape[3])
+            gate_sum[...] += jnp.dot(x, w, preferred_element_type=jnp.float32)
+            w = up_ref[:, j].reshape(depth, up_ref.shape[3])
+            up_sum[...] += jnp.dot(x, w, preferred_element_type=jnp.float32)
+
+    @pl.when(step == steps - 1)
+    def _():
+        hidden[...] = (jax.nn.silu(gate_sum[...]) * up_sum[...]).astype(jnp.bfloat16)
+
+    @pl.when(step >= steps)
+    def _():
+        y_ref[...] = jnp.dot(
+            hidden[...], out_ref[...], preferred_element_type=jnp.float32
+        ).astype(jnp.bfloat16)
+
+
+def run_expert(x, gate, up, out, ny, nk, per=2):
+    rows, width = x.shape
+    hid = gate.shape[1]
+    unit = width // (ny * nk)
+    steps = nk // per
+    cols = width // steps
+    first = lambda i: jnp.minimum(i, steps - 1)
+    second = lambda i: jnp.maximum(i - steps, 0)
+    w_spec = pl.BlockSpec((ny, per, unit, hid), lambda i: (0, first(i), 0, 0))
+    return pl.pallas_call(
+        functools.partial(expert_kernel, steps, per),
+        grid=(2 * steps,),
+        in_specs=[
+            pl.BlockSpec((rows, cols), lambda i: (0, first(i))),
+            w_spec,
+            w_spec,
+            pl.BlockSpec((hid, cols), lambda i: (0, second(i))),
+        ],
+        out_specs=pl.BlockSpec((rows, cols), lambda i: (0, second(i))),
+        out_shape=jax.ShapeDtypeStruct((rows, width), jnp.bfloat16),
+        scratch_shapes=[
+            pltpu.VMEM((rows, hid), jnp.float32),
+            pltpu.VMEM((rows, hid), jnp.float32),
+            pltpu.VMEM((rows, hid), jnp.bfloat16),
+        ],
+        compiler_params=pltpu.CompilerParams(vmem_limit_bytes=56 * 1024 * 1024),
+        cost_estimate=pl.CostEstimate(
+            flops=6 * rows * width * hid,
+            bytes_accessed=2 * (2 * rows * width + 3 * width * hid),
+            transcendentals=rows * hid,
+        ),
+    )(x, gate.reshape(ny, nk, unit, hid), up.reshape(ny, nk, unit, hid), out)
+
+
+def mix_kernel(per, x_ref, w_ref, o_ref, total):
+    step = pl.program_id(0)
+
+    @pl.when(step == 0)
+    def _():
+        total[...] = jnp.zeros_like(total)
+
+    for j in range(per):
+        w = w_ref[:, j].reshape(x_ref.shape[2], w_ref.shape[3])
+        total[...] += jnp.dot(x_ref[j], w, preferred_element_type=jnp.float32)
+
+    @pl.when(step == pl.num_programs(0) - 1)
+    def _():
+        o_ref[...] = total[...].astype(jnp.bfloat16)
+
+
+def run_mix(x, w, per=2):
+    ny, toks, depth = x.shape
+    nk, _, unit, cols = w.shape
+    return pl.pallas_call(
+        functools.partial(mix_kernel, per),
+        grid=(ny // per,),
+        in_specs=[
+            pl.BlockSpec((per, toks, depth), lambda i: (i, 0, 0)),
+            pl.BlockSpec((nk, per, unit, cols), lambda i: (0, i, 0, 0)),
+        ],
+        out_specs=pl.BlockSpec((toks, cols), lambda i: (0, 0)),
+        out_shape=jax.ShapeDtypeStruct((toks, cols), jnp.bfloat16),
+        scratch_shapes=[pltpu.VMEM((toks, cols), jnp.float32)],
+        compiler_params=pltpu.CompilerParams(vmem_limit_bytes=56 * 1024 * 1024),
+        cost_estimate=pl.CostEstimate(
+            flops=2 * ny * toks * depth * cols,
+            bytes_accessed=2 * ny * depth * cols,
+            transcendentals=0,
+        ),
+    )(x, w)
 
 
 def on_device(
@@ -54,8 +159,11 @@
     partial_latent = lax.dot_general(
         all_tokens, down_cols, (((1,), (1,)), ((), ())), preferred_element_type=jnp.float32
     )
+    partial_latent, select, targets = lax.optimization_barrier(
+        (partial_latent.astype(jnp.bfloat16), select, targets)
+    )
     pieces = lax.all_to_all(
-        partial_latent.astype(jnp.bfloat16).reshape(nr, tok_rows, ny * unit),
+        partial_latent.reshape(nr, tok_rows, ny * unit),
         "rep", split_axis=0, concat_axis=0, tiled=True,
     )
     latent = jnp.sum(pieces.astype(jnp.float32), axis=0).astype(jnp.bfloat16)
@@ -69,15 +177,7 @@
     full_rows = lax.all_gather(rows, "rep", axis=0, tiled=True)
     up_rows = spread(up_weight, "y")
 
-    def reorder(w):
-        return w.reshape(ny, nk, unit, w.shape[1]).transpose(1, 0, 2, 3).reshape(w.shape)
-
-    gate_act = jnp.dot(full_rows, reorder(gate_proj[0]), preferred_element_type=jnp.float32)
-    up_act = jnp.dot(full_rows, reorder(up_proj[0]), preferred_element_type=jnp.float32)
-    hidden = (jax.nn.silu(gate_act) * up_act).astype(jnp.bfloat16)
-    partial_out = jnp.dot(
-        hidden, out_proj[0], preferred_element_type=jnp.float32
-    ).astype(jnp.bfloat16)
+    partial_out = run_expert(full_rows, gate_proj[0], up_proj[0], out_proj[0], ny, nk)
     finished = lax.psum_scatter(partial_out, "rep", scatter_dimension=1, tiled=True)
     finished, up_rows = lax.optimization_barrier((finished, up_rows))
     all_up = lax.all_gather(up_rows, "k", axis=0, tiled=False)
@@ -89,10 +189,7 @@
     picked = returned.astype(jnp.float32).reshape(experts * capacity, slice_width)[targets]
     picked = picked.reshape(tok_rows, topk_count, slice_width)
     combined = jnp.sum(picked * route_gates[:, :, None], axis=1).astype(jnp.bfloat16)
-    full_latent = spread(combined, "rep").transpose(1, 0, 2).reshape(tok_rows, width)
-    all_up = all_up.transpose(1, 0, 2, 3).reshape(width, up_weight.shape[1])
-    mixed = jnp.dot(full_latent, all_up, preferred_element_type=jnp.float32)
-    return mixed.astype(jnp.bfloat16)
+    return run_mix(spread(combined, "rep"), all_up)
 
 
 def solution(mesh):

time: 269 us -> 264 us (0.981)
  blocking collectives: 72.6 us -> 95.8 us
  waiting for transfers between devices: 118 us -> 99.2 us
  matrix products: 17.4 us -> 2.86 us
  Pallas kernels: 0 us -> 13.1 us
  local copies, waits for them, and re-layouts: 18.3 us -> 12.8 us
  starting transfers between devices: 28.8 us -> 25.3 us
    all_to_all x0 -> x1, blocking collectives: none -> 24.3 us  [on_device(): lax.all_to_all(partial_latent.reshape(nr, tok_rows, ny * unit), 'rep', sp...]
    dot_general x3 -> x0, matrix products: 13.7 us -> none  [the longest x1 6.9 us: on_device(): jnp.dot(hidden, out_proj[0], preferred_element_type=jnp.float32)]
    pallas_call x0 -> x2, Pallas kernels: none -> 13.1 us  [the longest x1 8.65 us: run_expert(): pl.pallas_call(functools.partial(expert_kernel, steps, per), grid=(2 * st...]
    ppermute x1, waiting for transfers between devices: 9.83 us -> 0.01 us  [on_device(): sent_ids_t = lax.ppermute(ids_t, ('k', 'rep'), swap)]
    all_gather x1, waiting for transfers between devices: 15.6 us -> 6.78 us  [on_device(): all_tokens = lax.all_gather(tokens, 'k', axis=0, tiled=True)]
    all_to_all x1 -> x0, starting transfers between devices: 7.22 us -> none  [on_device(): lax.all_to_all(partial_latent.astype(jnp.bfloat16).reshape(nr, tok_rows,...]
    transpose x3 -> x0, local copies, waits for them, and re-layouts: 6.16 us -> none  [the longest x1 4.98 us: on_device(): all_up = all_up.transpose(1, 0, 2, 3).reshape(width, up_weight.shape[1])]
    all_gather x1, waiting for transfers between devices: 4.62 us -> 0.01 us  [on_device(): all_up = lax.all_gather(up_rows, 'k', axis=0, tiled=False)]
  transfers between devices with their start and end apart: 8 -> 7, of which waited for: 8 -> 5; matrix products, arithmetic and copies ran while one was open for 6% -> 5% of each run, Pallas kernels for 0% -> 0%
where the time goes in v2:
time: 264 us
  waiting for transfers between devices  99.2 us (38%)
  blocking collectives  95.8 us (36%)
  starting transfers between devices  25.3 us (10%)
  between operations  13.3 us (5%)
  Pallas kernels  13.1 us (5%)
  local copies, waits for them, and re-layouts  12.8 us (5%)
  matrix products  2.86 us (1%)
    all_to_all x2, blocking collectives, spread(): return lax.all_to_all(copies, axis, split_axis=0, concat_axis=0, tiled=True)  44.2 us
    all_gather x1, waiting for transfers between devices, on_device(): full_rows = lax.all_gather(rows, 'rep', axis=0, tiled=True)  39.7 us
    all_to_all x1, blocking collectives, on_device(): lax.all_to_all(send, ('y', 'k'), split_axis=0, concat_axis=0, tiled=True)  27.3 us
    all_to_all x1, blocking collectives, on_device(): lax.all_to_all(partial_latent.reshape(nr, tok_rows, ny * unit), 'rep', sp...  24.3 us
    reduce_scatter x1, waiting for transfers between devices, on_device(): lax.psum_scatter(partial_out, 'rep', scatter_dimension=1, tiled=True)  22.3 us
    all_to_all x1, waiting for transfers between devices, on_device(): lax.all_to_all(back.reshape(experts, capacity, slice_width), ('y', 'k'),...  17.7 us
    all_to_all x1, starting transfers between devices, on_device(): lax.all_to_all(back.reshape(experts, capacity, slice_width), ('y', 'k'),...  12.9 us
    all_to_all x1, waiting for transfers between devices, spread(): return lax.all_to_all(copies, axis, split_axis=0, concat_axis=0, tiled=True)  12 us
  transfers between devices with their start and end apart: 7, of which 5 were waited for; matrix products, arithmetic and copies ran while one was open for 5% of the time, Pallas kernels for 0%

profile of v2, /device:TPU:1, one launch (start us, length us, event | category | flops | bytes accessed | tf_op | source)
XLA Modules:
  0.0 263.6 jit_solution(2216658165512243860)
XLA Ops:
  6.5 0.7 all-gather.5.cloned.1.call-update
  7.3 5.4 %collective-permute-start = (s32[4,128]{1,0:T(4,128)}, s32[4,128]{1,0:T(4,128)S(1)}, u32[]{:S(2)}, u32[]{:S(2)}) collective-permute-start(s32[4,128]{1,0:T(4,128)} %bitcast.66), channel_id=1, source_target_pairs={{0,0},{1,8},{2,16},{3,24},{4,32},{5,40},{6,48},{7,56},{8,1},{9,9},... | collective-permute-start | bytes 6152 | tf_op jit(solution)/shard_map/ppermute | solution.py:148
  12.7 1.7 broadcast_in_dim.12
  14.4 6.8 %all-to-all-start = ((bf16[8,32,1024]{2,1,0:T(8,128)(2,1)}), bf16[8,32,1024]{2,1,0:T(8,128)(2,1)S(1)}, u32[]{:S(2)}, u32[]{:S(2)}) async-start(bf16[8,32,1024]{2,1,0:T(8,128)(2,1)} %broadcast_in_dim.12), calls=%async_computation | async-start | bytes 1048576 | tf_op jit(solution)/shard_map/all_to_all | solution.py:13
  21.2 0.8 slice_bitcast_fusion.3
  22.9 3.7 %gather_fusion.1 = s32[512]{0:T(512)S(1)} fusion(s32[64,128]{1,0:T(8,128)S(1)} %convolution_convert_fusion.2, s32[512]{0:T(512)S(1)} %fusion.18), kind=kCustom, calls=%fused_computation.1 | custom fusion | bytes 8192 | tf_op jit(solution)/shard_map/jit(take_along_axis)/gather | solution.py:156
  27.2 12.0 %all-to-all-done = bf16[8,32,1024]{2,1,0:T(8,128)(2,1)S(1)} async-done(((bf16[8,32,1024]{2,1,0:T(8,128)(2,1)}), bf16[8,32,1024]{2,1,0:T(8,128)(2,1)S(1)}, u32[]{:S(2)}, u32[]{:S(2)}) %all-to-all-start) | async-done | bytes 524320 | tf_op jit(solution)/shard_map/all_to_all | solution.py:13
  39.1 6.8 %all-gather.5.cloned.1.call-done = bf16[1024,1024]{1,0:T(8,128)(2,1)} async-done(((bf16[128,1024]{1,0:T(8,128)(2,1)}), bf16[1024,1024]{1,0:T(8,128)(2,1)}) %all-gather.5.cloned.1.call-update) | async-done | bytes 2097168 | tf_op jit(solution)/shard_map/all_gather | solution.py:150
  45.9 2.3 convolution_convert_fusion
  48.3 24.3 %all_to_all.30 = bf16[8,128,256]{2,1,0:T(8,128)(2,1)S(1)} all-to-all(bf16[8,128,256]{2,1,0:T(8,128)(2,1)S(1)} %bitcast.64), channel_id=1, replica_groups=mesh['y'=8,'k'=8,'rep'=8] {'rep'}, dimensions={0} | all-to-all | bytes 1048576 | tf_op jit(solution)/shard_map/all_to_all | solution.py:165
  73.1 27.3 %all_to_all.31 = bf16[64,12,256]{2,1,0:T(8,128)(2,1)S(1)} all-to-all(bf16[64,12,256]{2,1,0:T(8,128)(2,1)S(1)} %copy.17), channel_id=1, replica_groups=mesh['y'=8,'k'=8,'rep'=8] {'y','k'}, dimensions={0} | all-to-all | bytes 786432 | tf_op jit(solution)/shard_map/all_to_all | solution.py:173
  100.6 0.8 copy.22
  101.5 39.7 %all-gather.7.cloned.1.call-done.x_ref = bf16[768,2048]{1,0:T(8,128)(2,1)} async-done(((bf16[96,2048]{1,0:T(8,128)(2,1)}), bf16[768,2048]{1,0:T(8,128)(2,1)}) %all-gather.7.cloned.1.call-update) | async-done | bytes 3145744 | tf_op jit(solution)/shard_map/all_gather | solution.py:177
  141.1 8.6 %shard_map.82 = bf16[768,2048]{1,0:T(8,128)(2,1)} custom-call(bf16[768,2048]{1,0:T(8,128)(2,1)} %all-gather.7.cloned.1.call-done.x_ref, bf16[8,8,32,256]{3,2,1,0:T(8,128)(2,1)} %bitcast.60, bf16[8,8,32,256]{3,2,1,0:T(8,128)(2,1)} %bitcast.61, bf16[256,2048]{1,0:T(8,128)(2,1)} %bitcast.62), custom_call_target="tpu_custom_call" | custom-call | flops 2415919104 | bytes 9437184 | tf_op jit(solution)/shard_map/pallas_call | solution.py:71
  149.8 0.8 copy-done
  150.7 22.5 %all_to_all.32 = bf16[8,32,1024]{2,1,0:T(8,128)(2,1)} all-to-all(bf16[8,32,1024]{2,1,0:T(8,128)(2,1)S(1)} %broadcast_in_dim.14), channel_id=1, replica_groups=mesh['y'=8,'k'=8,'rep'=8] {'y'}, dimensions={0} | all-to-all | bytes 1048576 | tf_op jit(solution)/shard_map/all_to_all | solution.py:13
  173.1 22.3 %reduce-scatter.2.cloned.1.call-done = bf16[768,256]{1,0:T(8,128)(2,1)} async-done(((bf16[768,2048]{1,0:T(8,128)(2,1)}), bf16[768,256]{1,0:T(8,128)(2,1)}) %reduce-scatter.2.cloned.1.call-update) | async-done | bytes 393232 | tf_op jit(solution)/shard_map/reduce_scatter | solution.py:181
  195.5 1.1 reshape.113
  196.8 1.0 copy.20
  197.8 12.9 %all-to-all-start.4 = ((bf16[64,12,256]{2,1,0:T(8,128)(2,1)}), bf16[64,12,256]{2,1,0:T(8,128)(2,1)S(1)}, u32[]{:S(2)}, u32[]{:S(2)}) async-start(bf16[64,12,256]{2,1,0:T(8,128)(2,1)} %copy.20), calls=%async_computation.5 | async-start | bytes 1048576 | tf_op jit(solution)/shard_map/all_to_all | solution.py:185
  210.9 17.7 %all-to-all-done.4 = bf16[64,12,256]{2,1,0:T(8,128)(2,1)S(1)} async-done(((bf16[64,12,256]{2,1,0:T(8,128)(2,1)}), bf16[64,12,256]{2,1,0:T(8,128)(2,1)S(1)}, u32[]{:S(2)}, u32[]{:S(2)}) %all-to-all-start.4) | async-done | bytes 393248 | tf_op jit(solution)/shard_map/all_to_all | solution.py:185
  228.7 1.6 gather_fusion
  230.9 21.8 %all_to_all.33.x_ref = bf16[8,128,256]{2,1,0:T(8,128)(2,1)} all-to-all(bf16[8,128,256]{2,1,0:T(8,128)(2,1)S(1)} %broadcast_in_dim.16), channel_id=1, replica_groups=mesh['y'=8,'k'=8,'rep'=8] {'rep'}, dimensions={0} | all-to-all | bytes 1048576 | tf_op jit(solution)/shard_map/all_to_all | solution.py:13
  252.6 4.4 %shard_map.83 = bf16[128,1024]{1,0:T(8,128)(2,1)} custom-call(bf16[8,128,256]{2,1,0:T(8,128)(2,1)} %all_to_all.33.x_ref, bf16[8,8,32,1024]{3,2,1,0:T(8,128)(2,1)} %bitcast.54), custom_call_target="tpu_custom_call" | custom-call | flops 536870912 | bytes 4194304 | tf_op jit(solution)/shard_map/pallas_call | solution.py:115
  (36 shorter events, 3.2 us)
Async XLA Ops:
  6.5 39.4 %all-gather.5.cloned.1.call-start = ((), (), s32[]{:S(2)}) async-start(), calls=%async_computation.7 | async-start | bytes 2359296 | tf_op jit(solution)/shard_map/all_gather | solution.py:150
  7.3 19.4 %copy-start.1 = (s32[128,4]{0,1:T(4,128)S(1)}, s32[128,4]{0,1:T(4,128)}, u32[]{:S(2)}) copy-start(s32[128,4]{0,1:T(4,128)} %param.14) | copy-start | bytes 6148
  7.3 19.6 %collective-permute-start = (s32[4,128]{1,0:T(4,128)}, s32[4,128]{1,0:T(4,128)S(1)}, u32[]{:S(2)}, u32[]{:S(2)}) collective-permute-start(s32[4,128]{1,0:T(4,128)} %bitcast.66), channel_id=1, source_target_pairs={{0,0},{1,8},{2,16},{3,24},{4,32},{5,40},{6,48},{7,56},{8,1},{9,9},... | collective-permute-start | bytes 6152 | tf_op jit(solution)/shard_map/ppermute | solution.py:148
  14.4 24.8 %all-to-all-start = ((bf16[8,32,1024]{2,1,0:T(8,128)(2,1)}), bf16[8,32,1024]{2,1,0:T(8,128)(2,1)S(1)}, u32[]{:S(2)}, u32[]{:S(2)}) async-start(bf16[8,32,1024]{2,1,0:T(8,128)(2,1)} %broadcast_in_dim.12), calls=%async_computation | async-start | bytes 1048576 | tf_op jit(solution)/shard_map/all_to_all | solution.py:13
  21.2 119.9 %all-gather.7.cloned.1.call-start = ((), (), s32[]{:S(2)}) async-start(), calls=%async_computation.8 | async-start | bytes 3538944 | tf_op jit(solution)/shard_map/all_gather | solution.py:177
  101.4 94.1 %reduce-scatter.2.cloned.1.call-start = ((), (), s32[]{:S(2)}) async-start(), calls=%async_computation.9 | async-start | bytes 3538944 | tf_op jit(solution)/shard_map/reduce_scatter | solution.py:181
  149.8 0.8 copy-start
  149.8 102.8 %all-gather.9.cloned.1.call-start = ((), (), s32[]{:S(2)}) async-start(), calls=%async_computation.10 | async-start | bytes 4718592 | tf_op jit(solution)/shard_map/all_gather | solution.py:183
  173.1 37.7 %copy-start.2 = (f32[128,4]{0,1:T(4,128)S(1)}, f32[128,4]{0,1:T(4,128)}, u32[]{:S(2)}) copy-start(f32[128,4]{0,1:T(4,128)} %param.15) | copy-start | bytes 6148
  197.8 30.8 %all-to-all-start.4 = ((bf16[64,12,256]{2,1,0:T(8,128)(2,1)}), bf16[64,12,256]{2,1,0:T(8,128)(2,1)S(1)}, u32[]{:S(2)}, u32[]{:S(2)}) async-start(bf16[64,12,256]{2,1,0:T(8,128)(2,1)} %copy.20), calls=%async_computation.5 | async-start | bytes 1048576 | tf_op jit(solution)/shard_map/all_to_all | solution.py:185
Sparse Core Ops, SparseCore 0:
  9.5 36.3 all-gather.4
  101.5 39.5 all-gather.6
  149.9 45.5 reduce-scatter.1
  197.5 43.6 all-gather.8

commit v3 on v2

v3 whole, which is shorter than its diff:
```python
import functools

import jax
import jax.numpy as jnp
from jax import lax
from jax.experimental import pallas as pl
from jax.experimental.pallas import tpu as pltpu
from jax.sharding import Mesh, PartitionSpec as P


def spread(x, axis):
    copies = jnp.broadcast_to(x[None], (lax.axis_size(axis),) + x.shape)
    return lax.all_to_all(copies, axis, split_axis=0, concat_axis=0, tiled=True)


def expert_counts(ids_t, experts):
    tok = ids_t.shape[1]
    expert = lax.broadcasted_iota(jnp.int32, (experts, tok), 0)
    one_hot = jnp.zeros((experts, tok), jnp.bool_)
    for k in range(ids_t.shape[0]):
        one_hot = one_hot | (ids_t[k][None, :] == expert)
    earlier = lax.broadcasted_iota(jnp.int32, (tok, tok), 0) < lax.broadcasted_iota(
        jnp.int32, (tok, tok), 1
    )
    counts = jnp.dot(
        one_hot.astype(jnp.bfloat16),
        earlier.astype(jnp.bfloat16),
        preferred_element_type=jnp.float32,
    ).astype(jnp.int32)
    return one_hot, counts


def expert_kernel(x_ref, w_ref, out_ref, y_ref):
    hid = out_ref.shape[0]
    act = jnp.dot(x_ref[...], w_ref[...], preferred_element_type=jnp.float32)
    hidden = (jax.nn.silu(act[:, :hid]) * act[:, hid:]).astype(jnp.bfloat16)
    y_ref[...] = jnp.dot(
        hidden, out_ref[...], preferred_element_type=jnp.float32
    ).astype(jnp.bfloat16)


def run_expert(x, w, out, parts=3):
    rows, width = x.shape
    hid = out.shape[0]
    block = rows // parts
    return pl.pallas_call(
        expert_kernel,
        grid=(parts,),
        in_specs=[
            pl.BlockSpec((block, width), lambda i: (i, 0)),
            pl.BlockSpec((width, 2 * hid), lambda i: (0, 0)),
            pl.BlockSpec((hid, width), lambda i: (0, 0)),
        ],
        out_specs=pl.BlockSpec((block, width), lambda i: (i, 0)),
        out_shape=jax.ShapeDtypeStruct((rows, width), jnp.bfloat16),
        compiler_params=pltpu.CompilerParams(vmem_limit_bytes=56 * 1024 * 1024),
        cost_estimate=pl.CostEstimate(
            flops=6 * rows * width * hid,
            bytes_accessed=2 * (2 * rows * width + 3 * width * hid),
            transcendentals=rows * hid,
        ),
    )(x, w, out)


def mix_kernel(per, x_ref, w_ref, o_ref, total):
    step = pl.program_id(0)

    @pl.when(step == 0)
    def _():
        total[...] = jnp.zeros_like(total)

    for j in range(per):
        toks, depth = total.shape[0], 2 * x_ref.shape[2]
        x = jnp.concatenate([x_ref[j, :toks], x_ref[j, toks:]], axis=1)
        w = w_ref[:, j].reshape(depth, w_ref.shape[3])
        total[...] += jnp.dot(x, w, preferred_element_type=jnp.float32)

    @pl.when(step == pl.num_programs(0) - 1)
    def _():
        o_ref[...] = total[...].astype(jnp.bfloat16)


def run_mix(x, w, per=2):
    ny, toks, depth = x.shape[0], x.shape[1] // 2, 2 * x.shape[2]
    nk, _, unit, cols = w.shape
    return pl.pallas_call(
        functools.partial(mix_kernel, per),
        grid=(ny // per,),
        in_specs=[
            pl.BlockSpec((per, 2 * toks, depth // 2), lambda i: (i, 0, 0)),
            pl.BlockSpec((nk, per, unit, cols), lambda i: (0, i, 0, 0)),
        ],
        out_specs=pl.BlockSpec((toks, cols), lambda i: (0, 0)),
        out_shape=jax.ShapeDtypeStruct((toks, cols), jnp.bfloat16),
        scratch_shapes=[pltpu.VMEM((toks, cols), jnp.float32)],
        compiler_params=pltpu.CompilerParams(vmem_limit_bytes=56 * 1024 * 1024),
        cost_estimate=pl.CostEstimate(
            flops=2 * ny * toks * depth * cols,
            bytes_accessed=2 * ny * depth * cols,
            transcendentals=0,
        ),
    )(x, w)


def slot_mask(one_hot, counts, capacity):
    experts, toks = counts.shape
    shape = (experts, 2 * capacity, 2 * toks)
    row = lax.broadcasted_iota(jnp.int32, shape, 1)
    col = lax.broadcasted_iota(jnp.int32, shape, 2)
    row_half = (row >= capacity).astype(jnp.int32)
    col_half = (col >= toks).astype(jnp.int32)
    slot = jnp.where(one_hot, counts, -1)
    slot = jnp.concatenate([slot, slot], axis=1)[:, None, :]
    return (slot == row - capacity * row_half) & (row_half == col_half)


def combine_weights(ids_t, gates_t, experts, capacity):
    one_hot, counts = expert_counts(ids_t, experts)
    expert = lax.broadcasted_iota(jnp.int32, counts.shape, 0)
    gate = jnp.zeros(counts.shape, jnp.float32)
    for k in range(ids_t.shape[0]):
        gate = gate + jnp.where(ids_t[k][None, :] == expert, gates_t[k][None, :], 0.0)
    high = lax.reduce_precision(gate, 8, 7)
    mask = slot_mask(one_hot, counts, capacity)

    def spread_out(g):
        both = jnp.concatenate([g, g], axis=1)[:, None, :]
        return jnp.where(mask, both, 0.0).astype(jnp.bfloat16).reshape(-1, mask.shape[2])

    return spread_out(high), spread_out(gate - high)


def on_device(
    tokens, down_weight, gate_proj, up_proj, out_proj, up_weight, expert_ids, route_gates
):
    tok_rows = tokens.shape[0]
    topk_count = expert_ids.shape[1]
    ny, nk, nr = lax.axis_size("y"), lax.axis_size("k"), lax.axis_size("rep")
    experts = ny * nk
    capacity = max(2, 3 * tok_rows * topk_count // (2 * experts))
    width = gate_proj.shape[1]
    unit = down_weight.shape[1]
    slice_width = width // nr

    swap = [(i * nr + j, j * nr + i) for i in range(nk) for j in range(nr)]
    ids_t = expert_ids.T
    sent_ids_t = lax.ppermute(ids_t, ("k", "rep"), swap)

    all_tokens = lax.all_gather(tokens, "k", axis=0, tiled=True)
    down_cols = spread(down_weight.T, "y").reshape(ny * unit, down_weight.shape[0])
    one_hot, counts = expert_counts(sent_ids_t, experts)
    select = slot_mask(one_hot, counts, capacity).astype(jnp.bfloat16)
    select = select.reshape(2 * experts * capacity, 2 * tok_rows)

    partial_latent = lax.dot_general(
        all_tokens, down_cols, (((1,), (1,)), ((), ())), preferred_element_type=jnp.float32
    )
    partial_latent, select = lax.optimization_barrier(
        (partial_latent.astype(jnp.bfloat16), select)
    )
    pieces = lax.all_to_all(
        partial_latent.reshape(nr, tok_rows, ny * unit),
        "rep", split_axis=0, concat_axis=0, tiled=True,
    )
    latent = jnp.sum(pieces.astype(jnp.float32), axis=0).astype(jnp.bfloat16)
    half = ny * unit // 2
    latent = jnp.concatenate([latent[:, :half], latent[:, half:]], axis=0)
    send = jnp.dot(select, latent, preferred_element_type=jnp.float32).astype(jnp.bfloat16)
    got = lax.all_to_all(
        send.reshape(experts, 2 * capacity, half),
        ("y", "k"), split_axis=0, concat_axis=0, tiled=True,
    )
    rows = got.reshape(ny, nk, 2, capacity, half).transpose(3, 0, 1, 2, 4)
    rows = rows.reshape(capacity * ny, width)
    rows, up_weight = lax.optimization_barrier((rows, up_weight))
    full_rows = lax.all_gather(rows, "rep", axis=0, tiled=True)
    up_rows = spread(up_weight, "y")

    def reorder(w):
        return w.reshape(ny, nk, unit, w.shape[1]).transpose(1, 0, 2, 3).reshape(w.shape)

    high, low = combine_weights(expert_ids.T, route_gates.T, experts, capacity)
    weights = jnp.concatenate([reorder(gate_proj[0]), reorder(up_proj[0])], axis=1)
    full_rows, weights, high, low = lax.optimization_barrier((full_rows, weights, high, low))
    partial_out = run_expert(full_rows, weights, out_proj[0])
    finished = lax.psum_scatter(partial_out, "rep", scatter_dimension=1, tiled=True)
    finished, up_rows = lax.optimization_barrier((finished, up_rows))
    all_up = lax.all_gather(up_rows, "k", axis=0, tiled=False)
    back = finished.reshape(nr, capacity, ny, 2, slice_width // 2).transpose(2, 0, 3, 1, 4)
    returned = lax.all_to_all(
        back.reshape(experts, 2 * capacity, slice_width // 2),
        ("y", "k"), split_axis=0, concat_axis=0, tiled=True,
    )
    returned = returned.reshape(2 * experts * capacity, slice_width // 2)
    combined = sum(
        lax.dot_general(
            g, returned, (((0,), (0,)), ((), ())), preferred_element_type=jnp.float32
        )
        for g in (high, low)
    ).astype(jnp.bfloat16)
    return run_mix(spread(combined, "rep"), all_up)


def solution(mesh):
    nexp, nrep = mesh.devices.shape
    fine = Mesh(mesh.devices.reshape(nexp // nrep, nrep, nrep), ("y", "k", "rep"))
    exp = ("y", "k")
    in_specs = (
        P(exp, "rep"),
        P("rep", exp),
        P(exp, None, "rep"),
        P(exp, None, "rep"),
        P(exp, "rep", None),
        P(exp, "rep"),
        P(exp, None),
        P(exp, None),
    )
    return jax.shard_map(
        on_device, mesh=fine, in_specs=in_specs, out_specs=P(exp, "rep"), check_vma=False
    )
```

time: 264 us -> 255 us (0.966)
  blocking collectives: 95.8 us -> 122 us
  waiting for transfers between devices: 99.2 us -> 83.6 us
  starting transfers between devices: 25.3 us -> 12.3 us
  local copies, waits for them, and re-layouts: 12.8 us -> 5.91 us
    all_to_all x1 -> x2, blocking collectives: 27.3 us -> 52.3 us  [the longest x1 27.8 us: on_device(): lax.all_to_all(back.reshape(experts, 2 * capacity, slice_width // 2), ('y...]
    all_to_all x1 -> x0, waiting for transfers between devices: 17.7 us -> none  [on_device(): lax.all_to_all(back.reshape(experts, capacity, slice_width), ('y', 'k'),...]
    all_to_all x1 -> x0, starting transfers between devices: 12.9 us -> none  [on_device(): lax.all_to_all(back.reshape(experts, capacity, slice_width), ('y', 'k'),...]
    gather x2 -> x0, local copies, waits for them, and re-layouts: 5.31 us -> none  [the longest x1 3.74 us: on_device(): own_slot = jnp.take_along_axis(own_counts, ids_t, axis=0)]
    all_to_all x1, waiting for transfers between devices: 12 us -> 17 us  [spread(): return lax.all_to_all(copies, axis, split_axis=0, concat_axis=0, tiled=True)]
    all_gather x1, waiting for transfers between devices: 39.7 us -> 36.5 us  [on_device(): full_rows = lax.all_gather(rows, 'rep', axis=0, tiled=True)]
  transfers between devices with their start and end apart: 7 -> 6, of which waited for: 5 -> 4; matrix products, arithmetic and copies ran while one was open for 5% -> 3% of each run, Pallas kernels for 0% -> 0%
where the time goes in v3:
time: 255 us; the launch traced here: 254 us
  blocking collectives  122 us (48%)
  waiting for transfers between devices  83.6 us (33%)
  between operations  13.4 us (5%)
  starting transfers between devices  12.3 us (5%)
  Pallas kernels  11.3 us (4%)
  local copies, waits for them, and re-layouts  5.91 us (2%)
  matrix products  3.8 us (1%)
  other arithmetic  2.62 us (1%)
    all_to_all x2, blocking collectives, spread(): return lax.all_to_all(copies, axis, split_axis=0, concat_axis=0, tiled=True)  44.8 us
    all_gather x1, waiting for transfers between devices, on_device(): full_rows = lax.all_gather(rows, 'rep', axis=0, tiled=True)  36.5 us
    all_to_all x1, blocking collectives, on_device(): lax.all_to_all(back.reshape(experts, 2 * capacity, slice_width // 2), ('y...  27.8 us
    all_to_all x1, blocking collectives, on_device(): lax.all_to_all(send.reshape(experts, 2 * capacity, half), ('y', 'k'), spl...  24.6 us
    all_to_all x1, blocking collectives, on_device(): lax.all_to_all(partial_latent.reshape(nr, tok_rows, ny * unit), 'rep', sp...  24.3 us
    reduce_scatter x1, waiting for transfers between devices, on_device(): lax.psum_scatter(partial_out, 'rep', scatter_dimension=1, tiled=True)  22.5 us
    all_to_all x1, waiting for transfers between devices, spread(): return lax.all_to_all(copies, axis, split_axis=0, concat_axis=0, tiled=True)  17 us
    pallas_call x1, Pallas kernels, run_expert(): pl.pallas_call(expert_kernel, grid=(parts,), in_specs=[pl.BlockSpec((bloc...  6.91 us
  transfers between devices with their start and end apart: 6, of which 4 were waited for; matrix products, arithmetic and copies ran while one was open for 3% of the time, Pallas kernels for 0%

profile of v3, /device:TPU:1, one launch (start us, length us, event | category | flops | bytes accessed | tf_op | source)
XLA Modules:
  0.0 254.5 jit_solution(7806751045862241343)
XLA Ops:
  6.5 0.7 all-gather.5.cloned.1.call-update
  7.3 5.4 %collective-permute-start = (s32[4,128]{1,0:T(4,128)}, s32[4,128]{1,0:T(4,128)S(1)}, u32[]{:S(2)}, u32[]{:S(2)}) collective-permute-start(s32[4,128]{1,0:T(4,128)} %bitcast.94), channel_id=1, source_target_pairs={{0,0},{1,8},{2,16},{3,24},{4,32},{5,40},{6,48},{7,56},{8,1},{9,9},... | collective-permute-start | bytes 6152 | tf_op jit(solution)/shard_map/ppermute | solution.py:147
  12.7 1.7 broadcast_in_dim.87
  14.3 6.8 %all-to-all-start = ((bf16[8,32,1024]{2,1,0:T(8,128)(2,1)}), bf16[8,32,1024]{2,1,0:T(8,128)(2,1)S(1)}, u32[]{:S(2)}, u32[]{:S(2)}) async-start(bf16[8,32,1024]{2,1,0:T(8,128)(2,1)} %broadcast_in_dim.87), calls=%async_computation | async-start | bytes 1048576 | tf_op jit(solution)/shard_map/all_to_all | solution.py:13
  21.6 0.5 fusion.2
  22.1 17.0 %all-to-all-done = bf16[8,32,1024]{2,1,0:T(8,128)(2,1)S(1)} async-done(((bf16[8,32,1024]{2,1,0:T(8,128)(2,1)}), bf16[8,32,1024]{2,1,0:T(8,128)(2,1)S(1)}, u32[]{:S(2)}, u32[]{:S(2)}) %all-to-all-start) | async-done | bytes 524320 | tf_op jit(solution)/shard_map/all_to_all | solution.py:13
  39.1 6.8 %all-gather.5.cloned.1.call-done = bf16[1024,1024]{1,0:T(8,128)(2,1)} async-done(((bf16[128,1024]{1,0:T(8,128)(2,1)}), bf16[1024,1024]{1,0:T(8,128)(2,1)}) %all-gather.5.cloned.1.call-update) | async-done | bytes 2097168 | tf_op jit(solution)/shard_map/all_gather | solution.py:149
  46.0 2.3 convolution_convert_fusion.1
  48.3 24.3 %all_to_all.30 = bf16[8,128,256]{2,1,0:T(8,128)(2,1)S(1)} all-to-all(bf16[8,128,256]{2,1,0:T(8,128)(2,1)S(1)} %bitcast.91), channel_id=1, replica_groups=mesh['y'=8,'k'=8,'rep'=8] {'rep'}, dimensions={0} | all-to-all | bytes 1048576 | tf_op jit(solution)/shard_map/all_to_all | solution.py:161
  73.1 24.6 %all_to_all.31 = bf16[64,24,128]{2,1,0:T(8,128)(2,1)S(1)} all-to-all(bf16[64,24,128]{2,1,0:T(8,128)(2,1)S(1)} %bitcast.84), channel_id=1, replica_groups=mesh['y'=8,'k'=8,'rep'=8] {'y','k'}, dimensions={0} | all-to-all | bytes 786432 | tf_op jit(solution)/shard_map/all_to_all | solution.py:169
  97.8 0.8 copy.23
  99.7 0.5 fusion
  100.1 1.5 pad_maximum_fusion.w_ref
  101.7 36.5 %all-gather.7.cloned.1.call-done.x_ref = bf16[768,2048]{1,0:T(8,128)(2,1)} async-done(((bf16[96,2048]{1,0:T(8,128)(2,1)}), bf16[768,2048]{1,0:T(8,128)(2,1)}) %all-gather.7.cloned.1.call-update) | async-done | bytes 3145744 | tf_op jit(solution)/shard_map/all_gather | solution.py:176
  138.2 6.9 %shard_map.82 = bf16[768,2048]{1,0:T(8,128)(2,1)} custom-call(bf16[768,2048]{1,0:T(8,128)(2,1)} %all-gather.7.cloned.1.call-done.x_ref, bf16[2048,512]{1,0:T(8,128)(2,1)} %pad_maximum_fusion.w_ref, bf16[256,2048]{1,0:T(8,128)(2,1)} %bitcast.87), custom_call_target="tpu_custom_call" | custom-call | flops 2415919104 | bytes 9437184 | tf_op jit(solution)/shard_map/pallas_call | solution.py:46
  145.2 0.8 copy-done.2
  146.0 22.4 %all_to_all.32 = bf16[8,32,1024]{2,1,0:T(8,128)(2,1)} all-to-all(bf16[8,32,1024]{2,1,0:T(8,128)(2,1)S(1)} %broadcast_in_dim.103), channel_id=1, replica_groups=mesh['y'=8,'k'=8,'rep'=8] {'y'}, dimensions={0} | all-to-all | bytes 1048576 | tf_op jit(solution)/shard_map/all_to_all | solution.py:13
  168.4 22.5 %reduce-scatter.2.cloned.1.call-done = bf16[768,256]{1,0:T(8,128)(2,1)} async-done(((bf16[768,2048]{1,0:T(8,128)(2,1)}), bf16[768,256]{1,0:T(8,128)(2,1)}) %reduce-scatter.2.cloned.1.call-update) | async-done | bytes 393232 | tf_op jit(solution)/shard_map/reduce_scatter | solution.py:186
  190.9 1.3 copy.26
  192.4 27.8 %all_to_all.33 = bf16[64,24,128]{2,1,0:T(8,128)(2,1)S(1)} all-to-all(bf16[64,24,128]{2,1,0:T(8,128)(2,1)S(1)} %copy.27), channel_id=1, replica_groups=mesh['y'=8,'k'=8,'rep'=8] {'y','k'}, dimensions={0} | all-to-all | bytes 786432 | tf_op jit(solution)/shard_map/all_to_all | solution.py:190
  220.2 0.4 fusion.29
  220.6 0.4 fusion.3
  221.1 22.4 %all_to_all.34.x_ref = bf16[8,256,128]{2,1,0:T(8,128)(2,1)} all-to-all(bf16[8,256,128]{2,1,0:T(8,128)(2,1)S(1)} %broadcast_in_dim.104), channel_id=1, replica_groups=mesh['y'=8,'k'=8,'rep'=8] {'rep'}, dimensions={0} | all-to-all | bytes 1048576 | tf_op jit(solution)/shard_map/all_to_all | solution.py:13
  243.5 4.4 %shard_map.83 = bf16[128,1024]{1,0:T(8,128)(2,1)} custom-call(bf16[8,256,128]{2,1,0:T(8,128)(2,1)} %all_to_all.34.x_ref, bf16[8,8,32,1024]{3,2,1,0:T(8,128)(2,1)} %bitcast.78), custom_call_target="tpu_custom_call" | custom-call | flops 536870912 | bytes 4194304 | tf_op jit(solution)/shard_map/pallas_call | solution.py:86
  (43 shorter events, 2.4 us)
Async XLA Ops:
  6.5 39.4 %all-gather.5.cloned.1.call-start = ((), (), s32[]{:S(2)}) async-start(), calls=%async_computation.7 | async-start | bytes 2359296 | tf_op jit(solution)/shard_map/all_gather | solution.py:149
  7.3 14.2 %collective-permute-start = (s32[4,128]{1,0:T(4,128)}, s32[4,128]{1,0:T(4,128)S(1)}, u32[]{:S(2)}, u32[]{:S(2)}) collective-permute-start(s32[4,128]{1,0:T(4,128)} %bitcast.94), channel_id=1, source_target_pairs={{0,0},{1,8},{2,16},{3,24},{4,32},{5,40},{6,48},{7,56},{8,1},{9,9},... | collective-permute-start | bytes 6152 | tf_op jit(solution)/shard_map/ppermute | solution.py:147
  14.3 24.8 %all-to-all-start = ((bf16[8,32,1024]{2,1,0:T(8,128)(2,1)}), bf16[8,32,1024]{2,1,0:T(8,128)(2,1)S(1)}, u32[]{:S(2)}, u32[]{:S(2)}) async-start(bf16[8,32,1024]{2,1,0:T(8,128)(2,1)} %broadcast_in_dim.87), calls=%async_computation | async-start | bytes 1048576 | tf_op jit(solution)/shard_map/all_to_all | solution.py:13
  21.2 117.0 %all-gather.7.cloned.1.call-start = ((), (), s32[]{:S(2)}) async-start(), calls=%async_computation.8 | async-start | bytes 3538944 | tf_op jit(solution)/shard_map/all_gather | solution.py:176
  72.7 25.9 %copy-start = (bf16[1,2048,256]{2,1,0:T(8,128)(2,1)S(1)}, bf16[1,2048,256]{2,1,0:T(8,128)(2,1)}, u32[]{:S(2)}) copy-start(bf16[1,2048,256]{2,1,0:T(8,128)(2,1)} %param.10) | copy-start | bytes 3145732
  97.7 1.4 copy-start.1
  98.6 92.3 %reduce-scatter.2.cloned.1.call-start = ((), (), s32[]{:S(2)}) async-start(), calls=%async_computation.9 | async-start | bytes 3538944 | tf_op jit(solution)/shard_map/reduce_scatter | solution.py:186
  98.7 0.8 copy-start.3
  98.7 0.9 copy-start.4
  145.1 0.8 copy-start.2
  145.1 98.4 %all-gather.9.cloned.1.call-start = ((), (), s32[]{:S(2)}) async-start(), calls=%async_computation.10 | async-start | bytes 4718592 | tf_op jit(solution)/shard_map/all_gather | solution.py:188
Sparse Core Ops, SparseCore 0:
  9.5 36.4 all-gather.4
  98.7 39.4 all-gather.6
  145.3 45.5 reduce-scatter.1
  192.9 41.7 all-gather.8

commit v4 on v3

--- a/solution.py
+++ b/solution.py
@@ -34,12 +34,14 @@
     hid = out_ref.shape[0]
     act = jnp.dot(x_ref[...], w_ref[...], preferred_element_type=jnp.float32)
     hidden = (jax.nn.silu(act[:, :hid]) * act[:, hid:]).astype(jnp.bfloat16)
-    y_ref[...] = jnp.dot(
-        hidden, out_ref[...], preferred_element_type=jnp.float32
-    ).astype(jnp.bfloat16)
-
-
-def run_expert(x, w, out, parts=3):
+    chunk = min(512, y_ref.shape[1])
+    for c in range(0, y_ref.shape[1], chunk):
+        y_ref[:, c : c + chunk] = jnp.dot(
+            hidden, out_ref[:, c : c + chunk], preferred_element_type=jnp.float32
+        ).astype(jnp.bfloat16)
+
+
+def run_expert(x, w, out, parts=2):
     rows, width = x.shape
     hid = out.shape[0]
     block = rows // parts
@@ -80,7 +82,7 @@
         o_ref[...] = total[...].astype(jnp.bfloat16)
 
 
-def run_mix(x, w, per=2):
+def run_mix(x, w, per=4):
     ny, toks, depth = x.shape[0], x.shape[1] // 2, 2 * x.shape[2]
     nk, _, unit, cols = w.shape
     return pl.pallas_call(
@@ -142,12 +144,11 @@
     unit = down_weight.shape[1]
     slice_width = width // nr
 
-    swap = [(i * nr + j, j * nr + i) for i in range(nk) for j in range(nr)]
-    ids_t = expert_ids.T
-    sent_ids_t = lax.ppermute(ids_t, ("k", "rep"), swap)
-
     all_tokens = lax.all_gather(tokens, "k", axis=0, tiled=True)
     down_cols = spread(down_weight.T, "y").reshape(ny * unit, down_weight.shape[0])
+    swap = [(i * nr + j, j * nr + i) for i in range(nk) for j in range(nr)]
+    ids_t, _ = lax.optimization_barrier((expert_ids.T, down_cols))
+    sent_ids_t = lax.ppermute(ids_t, ("k", "rep"), swap)
     one_hot, counts = expert_counts(sent_ids_t, experts)
     select = slot_mask(one_hot, counts, capacity).astype(jnp.bfloat16)
     select = select.reshape(2 * experts * capacity, 2 * tok_rows)
@@ -155,11 +156,8 @@
     partial_latent = lax.dot_general(
         all_tokens, down_cols, (((1,), (1,)), ((), ())), preferred_element_type=jnp.float32
     )
-    partial_latent, select = lax.optimization_barrier(
-        (partial_latent.astype(jnp.bfloat16), select)
-    )
     pieces = lax.all_to_all(
-        partial_latent.reshape(nr, tok_rows, ny * unit),
+        partial_latent.astype(jnp.bfloat16).reshape(nr, tok_rows, ny * unit),
         "rep", split_axis=0, concat_axis=0, tiled=True,
     )
     latent = jnp.sum(pieces.astype(jnp.float32), axis=0).astype(jnp.bfloat16)

time: 255 us -> 256 us (level)
  blocking collectives: 122 us -> 98.1 us
  waiting for transfers between devices: 83.6 us -> 102 us
  starting transfers between devices: 12.3 us -> 18.9 us
    all_to_all x1 -> x0, blocking collectives: 24.3 us -> none  [on_device(): lax.all_to_all(partial_latent.reshape(nr, tok_rows, ny * unit), 'rep', sp...]
    ppermute x1, waiting for transfers between devices: 0.01 us -> 9.61 us  [on_device(): sent_ids_t = lax.ppermute(ids_t, ('k', 'rep'), swap)]
    all_gather x1, waiting for transfers between devices: 6.83 us -> 14.6 us  [on_device(): all_tokens = lax.all_gather(tokens, 'k', axis=0, tiled=True)]
    all_to_all x0 -> x1, starting transfers between devices: none -> 7.1 us  [on_device(): lax.all_to_all(partial_latent.astype(jnp.bfloat16).reshape(nr, tok_rows,...]
    all_to_all x0 -> x1, waiting for transfers between devices: none -> 3.38 us  [on_device(): lax.all_to_all(partial_latent.astype(jnp.bfloat16).reshape(nr, tok_rows,...]
  transfers between devices with their start and end apart: 6 -> 7, of which waited for: 4 -> 6; matrix products, arithmetic and copies ran while one was open for 3% -> 3% of each run, Pallas kernels for 0% -> 0%
where the time goes in v4:
time: 256 us
  waiting for transfers between devices  102 us (40%)
  blocking collectives  98.1 us (38%)
  starting transfers between devices  18.9 us (7%)
  between operations  13.3 us (5%)
  Pallas kernels  9.95 us (4%)
  local copies, waits for them, and re-layouts  5.74 us (2%)
  matrix products  4.63 us (2%)
  other arithmetic  2.63 us (1%)
    all_to_all x2, blocking collectives, spread(): return lax.all_to_all(copies, axis, split_axis=0, concat_axis=0, tiled=True)  44.6 us
    all_gather x1, waiting for transfers between devices, on_device(): full_rows = lax.all_gather(rows, 'rep', axis=0, tiled=True)  36.7 us
    all_to_all x1, blocking collectives, on_device(): lax.all_to_all(back.reshape(experts, 2 * capacity, slice_width // 2), ('y...  27.8 us
    all_to_all x1, blocking collectives, on_device(): lax.all_to_all(send.reshape(experts, 2 * capacity, half), ('y', 'k'), spl...  25.7 us
    reduce_scatter x1, waiting for transfers between devices, on_device(): lax.psum_scatter(partial_out, 'rep', scatter_dimension=1, tiled=True)  22.6 us
    all_to_all x1, waiting for transfers between devices, spread(): return lax.all_to_all(copies, axis, split_axis=0, concat_axis=0, tiled=True)  14.7 us
    all_gather x1, waiting for transfers between devices, on_device(): all_tokens = lax.all_gather(tokens, 'k', axis=0, tiled=True)  14.6 us
    ppermute x1, waiting for transfers between devices, on_device(): sent_ids_t = lax.ppermute(ids_t, ('k', 'rep'), swap)  9.61 us
  transfers between devices with their start and end apart: 7, of which 6 were waited for; matrix products, arithmetic and copies ran while one was open for 3% of the time, Pallas kernels for 0%

profile of v4, /device:TPU:1, one launch (start us, length us, event | category | flops | bytes accessed | tf_op | source)
XLA Modules:
  0.0 255.7 jit_solution(5399065106813426468)
XLA Ops:
  6.5 0.7 all-gather.5.cloned.1.call-update
  7.3 1.7 broadcast_in_dim.87
  8.9 7.7 %all-to-all-start = ((bf16[8,32,1024]{2,1,0:T(8,128)(2,1)}), bf16[8,32,1024]{2,1,0:T(8,128)(2,1)S(1)}, u32[]{:S(2)}, u32[]{:S(2)}) async-start(bf16[8,32,1024]{2,1,0:T(8,128)(2,1)} %broadcast_in_dim.87), calls=%async_computation | async-start | bytes 1048576 | tf_op jit(solution)/shard_map/all_to_all | solution.py:13
  16.6 14.7 %all-to-all-done = bf16[8,32,1024]{2,1,0:T(8,128)(2,1)S(1)} async-done(((bf16[8,32,1024]{2,1,0:T(8,128)(2,1)}), bf16[8,32,1024]{2,1,0:T(8,128)(2,1)S(1)}, u32[]{:S(2)}, u32[]{:S(2)}) %all-to-all-start) | async-done | bytes 524320 | tf_op jit(solution)/shard_map/all_to_all | solution.py:13
  31.3 14.6 %all-gather.5.cloned.1.call-done = bf16[1024,1024]{1,0:T(8,128)(2,1)} async-done(((bf16[128,1024]{1,0:T(8,128)(2,1)}), bf16[1024,1024]{1,0:T(8,128)(2,1)}) %all-gather.5.cloned.1.call-update) | async-done | bytes 2097168 | tf_op jit(solution)/shard_map/all_gather | solution.py:147
  45.9 3.1 %convolution_convert_fusion.1 = bf16[1024,256]{1,0:T(8,128)(2,1)} fusion(bf16[1024,1024]{1,0:T(8,128)(2,1)} %all-gather.5.cloned.1.call-done, bf16[256,1024]{1,0:T(8,128)(2,1)S(1)} %bitcast.88), kind=kOutput, calls=%fused_computation.10 | convolution fusion | flops 537133056 | bytes 3145728 | tf_op jit(solution)/shard_map/dot_general | solution.py:156
  49.1 7.1 %all-to-all-start.1 = ((bf16[8,128,256]{2,1,0:T(8,128)(2,1)}), bf16[8,128,256]{2,1,0:T(8,128)(2,1)S(1)}, u32[]{:S(2)}, u32[]{:S(2)}) async-start(bf16[8,128,256]{2,1,0:T(8,128)(2,1)} %bitcast.8), calls=%async_computation.1 | async-start | bytes 1048576 | tf_op jit(solution)/shard_map/all_to_all | solution.py:159
  56.2 4.0 %collective-permute-start = (s32[4,128]{1,0:T(4,128)S(1)}, s32[4,128]{1,0:T(4,128)S(1)}, u32[]{:S(2)}, u32[]{:S(2)}) collective-permute-start(s32[4,128]{1,0:T(4,128)S(1)} %bitcast.91), channel_id=1, source_target_pairs={{0,0},{1,8},{2,16},{3,24},{4,32},{5,40},{6,48},{7,56},{8,1},{9,9},... | collective-permute-start | bytes 6152 | tf_op jit(solution)/shard_map/ppermute | solution.py:151
  60.5 9.6 %collective-permute-done = s32[4,128]{1,0:T(4,128)S(1)} collective-permute-done((s32[4,128]{1,0:T(4,128)S(1)}, s32[4,128]{1,0:T(4,128)S(1)}, u32[]{:S(2)}, u32[]{:S(2)}) %collective-permute-start) | collective-permute-done | bytes 2080 | tf_op jit(solution)/shard_map/ppermute | solution.py:151
  70.2 0.5 compare_and_fusion.1
  70.7 3.4 %all-to-all-done.1 = bf16[8,128,256]{2,1,0:T(8,128)(2,1)S(1)} async-done(((bf16[8,128,256]{2,1,0:T(8,128)(2,1)}), bf16[8,128,256]{2,1,0:T(8,128)(2,1)S(1)}, u32[]{:S(2)}, u32[]{:S(2)}) %all-to-all-start.1) | async-done | bytes 524320 | tf_op jit(solution)/shard_map/all_to_all | solution.py:159
  74.6 25.7 %all_to_all.30 = bf16[64,24,128]{2,1,0:T(8,128)(2,1)S(1)} all-to-all(bf16[64,24,128]{2,1,0:T(8,128)(2,1)S(1)} %bitcast.84), channel_id=1, replica_groups=mesh['y'=8,'k'=8,'rep'=8] {'y','k'}, dimensions={0} | all-to-all | bytes 786432 | tf_op jit(solution)/shard_map/all_to_all | solution.py:167
  100.4 0.8 copy.23
  102.1 0.5 fusion
  102.6 1.5 pad_maximum_fusion.w_ref
  104.2 36.7 %all-gather.7.cloned.1.call-done.x_ref = bf16[768,2048]{1,0:T(8,128)(2,1)} async-done(((bf16[96,2048]{1,0:T(8,128)(2,1)}), bf16[768,2048]{1,0:T(8,128)(2,1)}) %all-gather.7.cloned.1.call-update) | async-done | bytes 3145744 | tf_op jit(solution)/shard_map/all_gather | solution.py:174
  140.9 6.4 %shard_map.82 = bf16[768,2048]{1,0:T(8,128)(2,1)} custom-call(bf16[768,2048]{1,0:T(8,128)(2,1)} %all-gather.7.cloned.1.call-done.x_ref, bf16[2048,512]{1,0:T(8,128)(2,1)} %pad_maximum_fusion.w_ref, bf16[256,2048]{1,0:T(8,128)(2,1)} %bitcast.85), custom_call_target="tpu_custom_call" | custom-call | flops 2415919104 | bytes 9437184 | tf_op jit(solution)/shard_map/pallas_call | solution.py:48
  147.3 0.8 copy-done.2
  148.1 22.4 %all_to_all.31 = bf16[8,32,1024]{2,1,0:T(8,128)(2,1)} all-to-all(bf16[8,32,1024]{2,1,0:T(8,128)(2,1)S(1)} %broadcast_in_dim.103), channel_id=1, replica_groups=mesh['y'=8,'k'=8,'rep'=8] {'y'}, dimensions={0} | all-to-all | bytes 1048576 | tf_op jit(solution)/shard_map/all_to_all | solution.py:13
  170.6 22.6 %reduce-scatter.2.cloned.1.call-done = bf16[768,256]{1,0:T(8,128)(2,1)} async-done(((bf16[768,2048]{1,0:T(8,128)(2,1)}), bf16[768,256]{1,0:T(8,128)(2,1)}) %reduce-scatter.2.cloned.1.call-update) | async-done | bytes 393232 | tf_op jit(solution)/shard_map/reduce_scatter | solution.py:184
  193.2 1.3 copy.26
  194.7 27.8 %all_to_all.32 = bf16[64,24,128]{2,1,0:T(8,128)(2,1)S(1)} all-to-all(bf16[64,24,128]{2,1,0:T(8,128)(2,1)S(1)} %copy.27), channel_id=1, replica_groups=mesh['y'=8,'k'=8,'rep'=8] {'y','k'}, dimensions={0} | all-to-all | bytes 786432 | tf_op jit(solution)/shard_map/all_to_all | solution.py:188
  223.4 22.2 %all_to_all.33.x_ref = bf16[8,256,128]{2,1,0:T(8,128)(2,1)} all-to-all(bf16[8,256,128]{2,1,0:T(8,128)(2,1)S(1)} %broadcast_in_dim.104), channel_id=1, replica_groups=mesh['y'=8,'k'=8,'rep'=8] {'rep'}, dimensions={0} | all-to-all | bytes 1048576 | tf_op jit(solution)/shard_map/all_to_all | solution.py:13
  245.6 3.6 %shard_map.83 = bf16[128,1024]{1,0:T(8,128)(2,1)} custom-call(bf16[8,256,128]{2,1,0:T(8,128)(2,1)} %all_to_all.33.x_ref, bf16[8,8,32,1024]{3,2,1,0:T(8,128)(2,1)} %bitcast.76), custom_call_target="tpu_custom_call" | custom-call | flops 536870912 | bytes 4194304 | tf_op jit(solution)/shard_map/pallas_call | solution.py:88
  (44 shorter events, 3.0 us)
Async XLA Ops:
  6.5 39.4 %all-gather.5.cloned.1.call-start = ((), (), s32[]{:S(2)}) async-start(), calls=%async_computation.7 | async-start | bytes 2359296 | tf_op jit(solution)/shard_map/all_gather | solution.py:147
  8.9 22.4 %all-to-all-start = ((bf16[8,32,1024]{2,1,0:T(8,128)(2,1)}), bf16[8,32,1024]{2,1,0:T(8,128)(2,1)S(1)}, u32[]{:S(2)}, u32[]{:S(2)}) async-start(bf16[8,32,1024]{2,1,0:T(8,128)(2,1)} %broadcast_in_dim.87), calls=%async_computation | async-start | bytes 1048576 | tf_op jit(solution)/shard_map/all_to_all | solution.py:13
  45.9 10.3 %copy-start.3 = (s32[128,4]{0,1:T(4,128)S(1)}, s32[128,4]{0,1:T(4,128)}, u32[]{:S(2)}) copy-start(s32[128,4]{0,1:T(4,128)} %param.14) | copy-start | bytes 6148
  49.1 25.1 %all-to-all-start.1 = ((bf16[8,128,256]{2,1,0:T(8,128)(2,1)}), bf16[8,128,256]{2,1,0:T(8,128)(2,1)S(1)}, u32[]{:S(2)}, u32[]{:S(2)}) async-start(bf16[8,128,256]{2,1,0:T(8,128)(2,1)} %bitcast.8), calls=%async_computation.1 | async-start | bytes 1048576 | tf_op jit(solution)/shard_map/all_to_all | solution.py:159
  56.2 84.7 %all-gather.7.cloned.1.call-start = ((), (), s32[]{:S(2)}) async-start(), calls=%async_computation.8 | async-start | bytes 3538944 | tf_op jit(solution)/shard_map/all_gather | solution.py:174
  56.2 13.8 %collective-permute-start = (s32[4,128]{1,0:T(4,128)S(1)}, s32[4,128]{1,0:T(4,128)S(1)}, u32[]{:S(2)}, u32[]{:S(2)}) collective-permute-start(s32[4,128]{1,0:T(4,128)S(1)} %bitcast.91), channel_id=1, source_target_pairs={{0,0},{1,8},{2,16},{3,24},{4,32},{5,40},{6,48},{7,56},{8,1},{9,9},... | collective-permute-start | bytes 6152 | tf_op jit(solution)/shard_map/ppermute | solution.py:151
  70.7 30.6 %copy-start = (bf16[1,2048,256]{2,1,0:T(8,128)(2,1)S(1)}, bf16[1,2048,256]{2,1,0:T(8,128)(2,1)}, u32[]{:S(2)}) copy-start(bf16[1,2048,256]{2,1,0:T(8,128)(2,1)} %param.10) | copy-start | bytes 3145732
  100.3 1.4 copy-start.1
  101.3 91.9 %reduce-scatter.2.cloned.1.call-start = ((), (), s32[]{:S(2)}) async-start(), calls=%async_computation.9 | async-start | bytes 3538944 | tf_op jit(solution)/shard_map/reduce_scatter | solution.py:184
  101.3 0.8 copy-start.4
  147.2 0.8 copy-start.2
  147.3 98.3 %all-gather.9.cloned.1.call-start = ((), (), s32[]{:S(2)}) async-start(), calls=%async_computation.10 | async-start | bytes 4718592 | tf_op jit(solution)/shard_map/all_gather | solution.py:186
Sparse Core Ops, SparseCore 0:
  9.5 36.3 all-gather.4
  101.4 39.4 all-gather.6
  147.4 45.7 reduce-scatter.1
  195.2 41.6 all-gather.8

commit v5 on v3

--- a/solution.py
+++ b/solution.py
@@ -34,25 +34,38 @@
     hid = out_ref.shape[0]
     act = jnp.dot(x_ref[...], w_ref[...], preferred_element_type=jnp.float32)
     hidden = (jax.nn.silu(act[:, :hid]) * act[:, hid:]).astype(jnp.bfloat16)
-    y_ref[...] = jnp.dot(
-        hidden, out_ref[...], preferred_element_type=jnp.float32
-    ).astype(jnp.bfloat16)
-
-
-def run_expert(x, w, out, parts=3):
-    rows, width = x.shape
+    pieces = y_ref.shape[0] if len(y_ref.shape) == 3 else 4
+    chunk = out_ref.shape[1] // pieces
+    for c in range(pieces):
+        y = jnp.dot(
+            hidden, out_ref[:, c * chunk : (c + 1) * chunk], preferred_element_type=jnp.float32
+        ).astype(jnp.bfloat16)
+        if len(y_ref.shape) == 3:
+            y_ref[c] = y
+        else:
+            y_ref[:, c * chunk : (c + 1) * chunk] = y
+
+
+def run_expert(x, w, out, block, first, parts, pieces=None):
+    width = x.shape[1]
     hid = out.shape[0]
-    block = rows // parts
+    rows = block * parts
+    if pieces is None:
+        out_spec = pl.BlockSpec((block, width), lambda i: (i, 0))
+        shape = (rows, width)
+    else:
+        out_spec = pl.BlockSpec((pieces, block, width // pieces), lambda i: (0, i, 0))
+        shape = (pieces, rows, width // pieces)
     return pl.pallas_call(
         expert_kernel,
         grid=(parts,),
         in_specs=[
-            pl.BlockSpec((block, width), lambda i: (i, 0)),
+            pl.BlockSpec((block, width), lambda i: (i + first, 0)),
             pl.BlockSpec((width, 2 * hid), lambda i: (0, 0)),
             pl.BlockSpec((hid, width), lambda i: (0, 0)),
         ],
-        out_specs=pl.BlockSpec((block, width), lambda i: (i, 0)),
-        out_shape=jax.ShapeDtypeStruct((rows, width), jnp.bfloat16),
+        out_specs=out_spec,
+        out_shape=jax.ShapeDtypeStruct(shape, jnp.bfloat16),
         compiler_params=pltpu.CompilerParams(vmem_limit_bytes=56 * 1024 * 1024),
         cost_estimate=pl.CostEstimate(
             flops=6 * rows * width * hid,
@@ -80,7 +93,7 @@
         o_ref[...] = total[...].astype(jnp.bfloat16)
 
 
-def run_mix(x, w, per=2):
+def run_mix(x, w, per=4):
     ny, toks, depth = x.shape[0], x.shape[1] // 2, 2 * x.shape[2]
     nk, _, unit, cols = w.shape
     return pl.pallas_call(
@@ -181,11 +194,23 @@
 
     high, low = combine_weights(expert_ids.T, route_gates.T, experts, capacity)
     weights = jnp.concatenate([reorder(gate_proj[0]), reorder(up_proj[0])], axis=1)
-    full_rows, weights, high, low = lax.optimization_barrier((full_rows, weights, high, low))
-    partial_out = run_expert(full_rows, weights, out_proj[0])
-    finished = lax.psum_scatter(partial_out, "rep", scatter_dimension=1, tiled=True)
-    finished, up_rows = lax.optimization_barrier((finished, up_rows))
+    full_rows, weights, high, low, up_rows = lax.optimization_barrier(
+        (full_rows, weights, high, low, up_rows)
+    )
+    per_source = capacity * ny
+    late = 3 * nr // 8
+    early_rows = (nr - late) * per_source
+    early_out = run_expert(full_rows, weights, out_proj[0], early_rows // 2, 0, 2)
+    late_in, early_out = lax.optimization_barrier((full_rows, early_out))
+    late_out = run_expert(
+        late_in, weights, out_proj[0], per_source, nr - late, late, pieces=nr
+    )
+    finished = lax.psum_scatter(early_out, "rep", scatter_dimension=1, tiled=True)
+    late_terms = lax.all_to_all(late_out, "rep", split_axis=0, concat_axis=0, tiled=True)
+    late_sum = jnp.sum(late_terms.astype(jnp.float32), axis=0).astype(jnp.bfloat16)
+    finished, up_rows, late_sum = lax.optimization_barrier((finished, up_rows, late_sum))
     all_up = lax.all_gather(up_rows, "k", axis=0, tiled=False)
+    finished = jnp.concatenate([finished, late_sum], axis=0)
     back = finished.reshape(nr, capacity, ny, 2, slice_width // 2).transpose(2, 0, 3, 1, 4)
     returned = lax.all_to_all(
         back.reshape(experts, 2 * capacity, slice_width // 2),

time: 255 us -> 266 us (1.043)
  blocking collectives: 122 us -> 144 us
  waiting for transfers between devices: 83.6 us -> 63.4 us
  starting transfers between devices: 12.3 us -> 16.1 us
  Pallas kernels: 11.3 us -> 14.2 us
    all_to_all x0 -> x1, blocking collectives: none -> 45 us  [on_device(): lax.all_to_all(late_out, 'rep', split_axis=0, concat_axis=0, tiled=True)]
    all_to_all x2 -> x1, blocking collectives: 44.8 us -> 23.4 us  [spread(): return lax.all_to_all(copies, axis, split_axis=0, concat_axis=0, tiled=True)]
    all_gather x1, waiting for transfers between devices: 36.5 us -> 16.5 us  [on_device(): full_rows = lax.all_gather(rows, 'rep', axis=0, tiled=True)]
    reduce_scatter x1, waiting for transfers between devices: 22.5 us -> 7.84 us  [on_device(): lax.psum_scatter(early_out, 'rep', scatter_dimension=1, tiled=True)]
    all_gather x1, waiting for transfers between devices: 6.83 us -> 14.6 us  [on_device(): all_tokens = lax.all_gather(tokens, 'k', axis=0, tiled=True)]
    all_to_all x1 -> x2, waiting for transfers between devices: 17 us -> 22.2 us  [spread(): return lax.all_to_all(copies, axis, split_axis=0, concat_axis=0, tiled=True)]
    all_to_all x1 -> x2, starting transfers between devices: 6.82 us -> 11.1 us  [spread(): return lax.all_to_all(copies, axis, split_axis=0, concat_axis=0, tiled=True)]
    pallas_call x1 -> x2, Pallas kernels: 6.91 us -> 10.6 us  [run_expert(): pl.pallas_call(expert_kernel, grid=(parts,), in_specs=[pl.BlockSpec((bloc...]
  transfers between devices with their start and end apart: 6 -> 7, of which waited for: 4 -> 6; matrix products, arithmetic and copies ran while one was open for 3% -> 4% of each run, Pallas kernels for 0% -> 2%
where the time goes in v5:
time: 266 us; the launch traced here: 265 us
  blocking collectives  144 us (54%)
  waiting for transfers between devices  63.4 us (24%)
  starting transfers between devices  16.1 us (6%)
  Pallas kernels  14.2 us (5%)
  between operations  13.4 us (5%)
  local copies, waits for them, and re-layouts  4.99 us (2%)
  other arithmetic  4.78 us (2%)
  matrix products  3.8 us (1%)
    all_to_all x1, blocking collectives, on_device(): lax.all_to_all(late_out, 'rep', split_axis=0, concat_axis=0, tiled=True)  45 us
    all_to_all x1, blocking collectives, on_device(): lax.all_to_all(back.reshape(experts, 2 * capacity, slice_width // 2), ('y...  26.9 us
    all_to_all x1, blocking collectives, on_device(): lax.all_to_all(partial_latent.reshape(nr, tok_rows, ny * unit), 'rep', sp...  24.5 us
    all_to_all x1, blocking collectives, on_device(): lax.all_to_all(send.reshape(experts, 2 * capacity, half), ('y', 'k'), spl...  24.5 us
    all_to_all x1, blocking collectives, spread(): return lax.all_to_all(copies, axis, split_axis=0, concat_axis=0, tiled=True)  23.4 us
    all_to_all x2, waiting for transfers between devices, spread(): return lax.all_to_all(copies, axis, split_axis=0, concat_axis=0, tiled=True)  22.2 us
    all_gather x1, waiting for transfers between devices, on_device(): full_rows = lax.all_gather(rows, 'rep', axis=0, tiled=True)  16.5 us
    all_gather x1, waiting for transfers between devices, on_device(): all_tokens = lax.all_gather(tokens, 'k', axis=0, tiled=True)  14.6 us
  transfers between devices with their start and end apart: 7, of which 6 were waited for; matrix products, arithmetic and copies ran while one was open for 4% of the time, Pallas kernels for 2%

profile of v5, /device:TPU:1, one launch (start us, length us, event | category | flops | bytes accessed | tf_op | source)
XLA Modules:
  0.0 264.9 jit_solution(11434180172944706075)
XLA Ops:
  7.3 1.7 broadcast_in_dim.87
  8.9 7.7 %all-to-all-start = ((bf16[8,32,1024]{2,1,0:T(8,128)(2,1)}), bf16[8,32,1024]{2,1,0:T(8,128)(2,1)S(1)}, u32[]{:S(2)}, u32[]{:S(2)}) async-start(bf16[8,32,1024]{2,1,0:T(8,128)(2,1)} %broadcast_in_dim.87), calls=%async_computation | async-start | bytes 1048576 | tf_op jit(solution)/shard_map/all_to_all | solution.py:13
  16.6 4.8 %collective-permute-start = (s32[4,128]{1,0:T(4,128)}, s32[4,128]{1,0:T(4,128)S(1)}, u32[]{:S(2)}, u32[]{:S(2)}) collective-permute-start(s32[4,128]{1,0:T(4,128)} %bitcast.95), channel_id=1, source_target_pairs={{0,0},{1,8},{2,16},{3,24},{4,32},{5,40},{6,48},{7,56},{8,1},{9,9},... | collective-permute-start | bytes 6152 | tf_op jit(solution)/shard_map/ppermute | solution.py:160
  21.7 1.5 collective-permute-done
  23.9 7.5 %all-to-all-done = bf16[8,32,1024]{2,1,0:T(8,128)(2,1)S(1)} async-done(((bf16[8,32,1024]{2,1,0:T(8,128)(2,1)}), bf16[8,32,1024]{2,1,0:T(8,128)(2,1)S(1)}, u32[]{:S(2)}, u32[]{:S(2)}) %all-to-all-start) | async-done | bytes 524320 | tf_op jit(solution)/shard_map/all_to_all | solution.py:13
  31.3 14.6 %all-gather.5.cloned.1.call-done = bf16[1024,1024]{1,0:T(8,128)(2,1)} async-done(((bf16[128,1024]{1,0:T(8,128)(2,1)}), bf16[1024,1024]{1,0:T(8,128)(2,1)}) %all-gather.5.cloned.1.call-update) | async-done | bytes 2097168 | tf_op jit(solution)/shard_map/all_gather | solution.py:162
  45.9 2.3 convolution_convert_fusion.1
  48.3 24.5 %all_to_all.35 = bf16[8,128,256]{2,1,0:T(8,128)(2,1)S(1)} all-to-all(bf16[8,128,256]{2,1,0:T(8,128)(2,1)S(1)} %bitcast.93), channel_id=1, replica_groups=mesh['y'=8,'k'=8,'rep'=8] {'rep'}, dimensions={0} | all-to-all | bytes 1048576 | tf_op jit(solution)/shard_map/all_to_all | solution.py:174
  73.2 24.5 %all_to_all.36 = bf16[64,24,128]{2,1,0:T(8,128)(2,1)S(1)} all-to-all(bf16[64,24,128]{2,1,0:T(8,128)(2,1)S(1)} %bitcast.86), channel_id=1, replica_groups=mesh['y'=8,'k'=8,'rep'=8] {'y','k'}, dimensions={0} | all-to-all | bytes 786432 | tf_op jit(solution)/shard_map/all_to_all | solution.py:182
  97.8 0.8 copy.23
  99.6 0.9 broadcast_in_dim.103
  100.4 3.5 %all-to-all-start.3 = ((bf16[8,32,1024]{2,1,0:T(8,128)(2,1)}), bf16[8,32,1024]{2,1,0:T(8,128)(2,1)S(1)}, u32[]{:S(2)}, u32[]{:S(2)}) async-start(bf16[8,32,1024]{2,1,0:T(8,128)(2,1)} %broadcast_in_dim.103), calls=%async_computation.3 | async-start | bytes 1048576 | tf_op jit(solution)/shard_map/all_to_all | solution.py:13
  104.1 1.4 fusion
  105.5 1.5 pad_maximum_fusion.w_ref
  107.0 14.8 %all-to-all-done.3 = bf16[8,32,1024]{2,1,0:T(8,128)(2,1)S(1)} async-done(((bf16[8,32,1024]{2,1,0:T(8,128)(2,1)}), bf16[8,32,1024]{2,1,0:T(8,128)(2,1)S(1)}, u32[]{:S(2)}, u32[]{:S(2)}) %all-to-all-start.3) | async-done | bytes 524320 | tf_op jit(solution)/shard_map/all_to_all | solution.py:13
  121.8 16.5 %all-gather.7.cloned.1.call-done.x_ref = bf16[768,2048]{1,0:T(8,128)(2,1)} async-done(((bf16[96,2048]{1,0:T(8,128)(2,1)}), bf16[768,2048]{1,0:T(8,128)(2,1)}) %all-gather.7.cloned.1.call-update) | async-done | bytes 3145744 | tf_op jit(solution)/shard_map/all_gather | solution.py:189
  138.3 5.2 %shard_map.82 = bf16[480,2048]{1,0:T(8,128)(2,1)} custom-call(bf16[768,2048]{1,0:T(8,128)(2,1)} %all-gather.7.cloned.1.call-done.x_ref, bf16[2048,512]{1,0:T(8,128)(2,1)} %pad_maximum_fusion.w_ref, bf16[256,2048]{1,0:T(8,128)(2,1)} %bitcast.81), custom_call_target="tpu_custom_call" | custom-call | flops 1509949440 | bytes 7077888 | tf_op jit(solution)/shard_map/pallas_call | solution.py:59
  143.6 5.4 %shard_map.83 = bf16[8,288,256]{2,1,0:T(8,128)(2,1)} custom-call(bf16[768,2048]{1,0:T(8,128)(2,1)} %all-gather.7.cloned.1.call-done.x_ref, bf16[2048,512]{1,0:T(8,128)(2,1)} %pad_maximum_fusion.w_ref, bf16[256,2048]{1,0:T(8,128)(2,1)} %bitcast.82), custom_call_target="tpu_custom_call" | custom-call | flops 905969664 | bytes 5505024 | tf_op jit(solution)/shard_map/pallas_call | solution.py:59
  149.0 45.0 %all_to_all.37 = bf16[8,288,256]{2,1,0:T(8,128)(2,1)S(1)} all-to-all(bf16[8,288,256]{2,1,0:T(8,128)(2,1)} %shard_map.83), channel_id=1, replica_groups=mesh['y'=8,'k'=8,'rep'=8] {'rep'}, dimensions={0} | all-to-all | bytes 2359296 | tf_op jit(solution)/shard_map/all_to_all | solution.py:209
  194.1 7.8 %reduce-scatter.2.cloned.1.call-done = bf16[480,256]{1,0:T(8,128)(2,1)} async-done(((bf16[480,2048]{1,0:T(8,128)(2,1)}), bf16[480,256]{1,0:T(8,128)(2,1)}) %reduce-scatter.2.cloned.1.call-update) | async-done | bytes 245776 | tf_op jit(solution)/shard_map/reduce_scatter | solution.py:208
  202.0 1.0 pad_maximum_fusion.1
  203.6 26.9 %all_to_all.38 = bf16[64,24,128]{2,1,0:T(8,128)(2,1)S(1)} all-to-all(bf16[64,24,128]{2,1,0:T(8,128)(2,1)S(1)} %copy.27), channel_id=1, replica_groups=mesh['y'=8,'k'=8,'rep'=8] {'y','k'}, dimensions={0} | all-to-all | bytes 786432 | tf_op jit(solution)/shard_map/all_to_all | solution.py:215
  231.4 23.4 %all_to_all.39.x_ref = bf16[8,256,128]{2,1,0:T(8,128)(2,1)} all-to-all(bf16[8,256,128]{2,1,0:T(8,128)(2,1)S(1)} %broadcast_in_dim.104), channel_id=1, replica_groups=mesh['y'=8,'k'=8,'rep'=8] {'rep'}, dimensions={0} | all-to-all | bytes 1048576 | tf_op jit(solution)/shard_map/all_to_all | solution.py:13
  254.8 3.6 %shard_map.84 = bf16[128,1024]{1,0:T(8,128)(2,1)} custom-call(bf16[8,256,128]{2,1,0:T(8,128)(2,1)} %all_to_all.39.x_ref, bf16[8,8,32,1024]{3,2,1,0:T(8,128)(2,1)} %bitcast.78), custom_call_target="tpu_custom_call" | custom-call | flops 536870912 | bytes 4194304 | tf_op jit(solution)/shard_map/pallas_call | solution.py:99
  (52 shorter events, 4.8 us)
Async XLA Ops:
  6.5 39.4 %all-gather.5.cloned.1.call-start = ((), (), s32[]{:S(2)}) async-start(), calls=%async_computation.8 | async-start | bytes 2359296 | tf_op jit(solution)/shard_map/all_gather | solution.py:162
  8.9 22.4 %all-to-all-start = ((bf16[8,32,1024]{2,1,0:T(8,128)(2,1)}), bf16[8,32,1024]{2,1,0:T(8,128)(2,1)S(1)}, u32[]{:S(2)}, u32[]{:S(2)}) async-start(bf16[8,32,1024]{2,1,0:T(8,128)(2,1)} %broadcast_in_dim.87), calls=%async_computation | async-start | bytes 1048576 | tf_op jit(solution)/shard_map/all_to_all | solution.py:13
  16.6 121.7 %all-gather.7.cloned.1.call-start = ((), (), s32[]{:S(2)}) async-start(), calls=%async_computation.9 | async-start | bytes 3538944 | tf_op jit(solution)/shard_map/all_gather | solution.py:189
  16.6 6.6 %collective-permute-start = (s32[4,128]{1,0:T(4,128)}, s32[4,128]{1,0:T(4,128)S(1)}, u32[]{:S(2)}, u32[]{:S(2)}) collective-permute-start(s32[4,128]{1,0:T(4,128)} %bitcast.95), channel_id=1, source_target_pairs={{0,0},{1,8},{2,16},{3,24},{4,32},{5,40},{6,48},{7,56},{8,1},{9,9},... | collective-permute-start | bytes 6152 | tf_op jit(solution)/shard_map/ppermute | solution.py:160
  72.8 25.8 %copy-start.2 = (bf16[1,2048,256]{2,1,0:T(8,128)(2,1)S(1)}, bf16[1,2048,256]{2,1,0:T(8,128)(2,1)}, u32[]{:S(2)}) copy-start(bf16[1,2048,256]{2,1,0:T(8,128)(2,1)} %param.11) | copy-start | bytes 3145732
  97.7 1.4 copy-start.3
  98.6 0.8 copy-start.5
  98.6 0.9 copy-start.4
  98.8 5.2 %copy-start.6 = (f32[128,4]{0,1:T(4,128)S(1)}, f32[128,4]{0,1:T(4,128)}, u32[]{:S(2)}) copy-start(f32[128,4]{0,1:T(4,128)} %param.15) | copy-start | bytes 6148
  100.4 21.4 %all-to-all-start.3 = ((bf16[8,32,1024]{2,1,0:T(8,128)(2,1)}), bf16[8,32,1024]{2,1,0:T(8,128)(2,1)S(1)}, u32[]{:S(2)}, u32[]{:S(2)}) async-start(bf16[8,32,1024]{2,1,0:T(8,128)(2,1)} %broadcast_in_dim.103), calls=%async_computation.3 | async-start | bytes 1048576 | tf_op jit(solution)/shard_map/all_to_all | solution.py:13
  103.9 98.1 %reduce-scatter.2.cloned.1.call-start = ((), (), s32[]{:S(2)}) async-start(), calls=%async_computation.10 | async-start | bytes 2211840 | tf_op jit(solution)/shard_map/reduce_scatter | solution.py:208
  121.8 21.7 %copy-start.1 = (bf16[8,32,1024]{2,1,0:T(8,128)(2,1)}, bf16[8,32,1024]{2,1,0:T(8,128)(2,1)S(1)}, u32[]{:S(2)}) copy-start(bf16[8,32,1024]{2,1,0:T(8,128)(2,1)S(1)} %all-to-all-done.3) | copy-start | bytes 1572868
  143.5 111.3 %all-gather.9.cloned.1.call-start = ((), (), s32[]{:S(2)}) async-start(), calls=%async_computation.11 | async-start | bytes 4718592 | tf_op jit(solution)/shard_map/all_gather | solution.py:212
  202.0 28.9 %copy-start = (bf16[1536,256]{1,0:T(8,128)(2,1)S(1)}, bf16[1536,256]{1,0:T(8,128)(2,1)}, u32[]{:S(2)}) copy-start(bf16[1536,256]{1,0:T(8,128)(2,1)} %get-tuple-element.31) | copy-start | bytes 2359300
Sparse Core Ops, SparseCore 0:
  9.5 36.3 all-gather.4
  98.7 39.4 all-gather.6
  143.6 58.2 reduce-scatter.1
  204.2 41.2 all-gather.8

commit v6 on v4

--- a/solution.py
+++ b/solution.py
@@ -144,11 +144,12 @@
     unit = down_weight.shape[1]
     slice_width = width // nr
 
+    swap = [(i * nr + j, j * nr + i) for i in range(nk) for j in range(nr)]
+    ids_t = expert_ids.T
+    sent_ids_t = lax.ppermute(ids_t, ("k", "rep"), swap)
+
     all_tokens = lax.all_gather(tokens, "k", axis=0, tiled=True)
     down_cols = spread(down_weight.T, "y").reshape(ny * unit, down_weight.shape[0])
-    swap = [(i * nr + j, j * nr + i) for i in range(nk) for j in range(nr)]
-    ids_t, _ = lax.optimization_barrier((expert_ids.T, down_cols))
-    sent_ids_t = lax.ppermute(ids_t, ("k", "rep"), swap)
     one_hot, counts = expert_counts(sent_ids_t, experts)
     select = slot_mask(one_hot, counts, capacity).astype(jnp.bfloat16)
     select = select.reshape(2 * experts * capacity, 2 * tok_rows)
@@ -156,8 +157,11 @@
     partial_latent = lax.dot_general(
         all_tokens, down_cols, (((1,), (1,)), ((), ())), preferred_element_type=jnp.float32
     )
+    partial_latent, select = lax.optimization_barrier(
+        (partial_latent.astype(jnp.bfloat16), select)
+    )
     pieces = lax.all_to_all(
-        partial_latent.astype(jnp.bfloat16).reshape(nr, tok_rows, ny * unit),
+        partial_latent.reshape(nr, tok_rows, ny * unit),
         "rep", split_axis=0, concat_axis=0, tiled=True,
     )
     latent = jnp.sum(pieces.astype(jnp.float32), axis=0).astype(jnp.bfloat16)
@@ -179,7 +183,9 @@
 
     high, low = combine_weights(expert_ids.T, route_gates.T, experts, capacity)
     weights = jnp.concatenate([reorder(gate_proj[0]), reorder(up_proj[0])], axis=1)
-    full_rows, weights, high, low = lax.optimization_barrier((full_rows, weights, high, low))
+    full_rows, weights, high, low, up_rows = lax.optimization_barrier(
+        (full_rows, weights, high, low, up_rows)
+    )
     partial_out = run_expert(full_rows, weights, out_proj[0])
     finished = lax.psum_scatter(partial_out, "rep", scatter_dimension=1, tiled=True)
     finished, up_rows = lax.optimization_barrier((finished, up_rows))

time: 256 us -> 254 us (level)
  starting transfers between devices: 18.9 us -> 15.8 us
    all_to_all x0 -> x1, blocking collectives: none -> 24.5 us  [on_device(): lax.all_to_all(partial_latent.reshape(nr, tok_rows, ny * unit), 'rep', sp...]
    reduce_scatter x1, waiting for transfers between devices: 22.6 us -> 45.9 us  [on_device(): lax.psum_scatter(partial_out, 'rep', scatter_dimension=1, tiled=True)]
    all_to_all x2 -> x1, blocking collectives: 44.6 us -> 22.3 us  [spread(): return lax.all_to_all(copies, axis, split_axis=0, concat_axis=0, tiled=True)]
    all_gather x1, waiting for transfers between devices: 36.7 us -> 16.5 us  [on_device(): full_rows = lax.all_gather(rows, 'rep', axis=0, tiled=True)]
    all_to_all x1 -> x2, waiting for transfers between devices: 14.7 us -> 31.8 us  [spread(): return lax.all_to_all(copies, axis, split_axis=0, concat_axis=0, tiled=True)]
    ppermute x1, waiting for transfers between devices: 9.61 us -> 0.01 us  [on_device(): sent_ids_t = lax.ppermute(ids_t, ('k', 'rep'), swap)]
    all_gather x1, waiting for transfers between devices: 14.6 us -> 6.83 us  [on_device(): all_tokens = lax.all_gather(tokens, 'k', axis=0, tiled=True)]
    all_to_all x1 -> x0, starting transfers between devices: 7.1 us -> none  [on_device(): lax.all_to_all(partial_latent.astype(jnp.bfloat16).reshape(nr, tok_rows,...]
  transfers between devices with their start and end apart: 7 -> 7, of which waited for: 6 -> 5; matrix products, arithmetic and copies ran while one was open for 3% -> 4% of each run, Pallas kernels for 0% -> 0%
where the time goes in v6:
time: 254 us; the launch traced here: 253 us
  waiting for transfers between devices  102 us (40%)
  blocking collectives  98.9 us (39%)
  starting transfers between devices  15.8 us (6%)
  between operations  13.4 us (5%)
  Pallas kernels  10 us (4%)
  local copies, waits for them, and re-layouts  5.96 us (2%)
  matrix products  3.81 us (2%)
  other arithmetic  3.61 us (1%)
    reduce_scatter x1, waiting for transfers between devices, on_device(): lax.psum_scatter(partial_out, 'rep', scatter_dimension=1, tiled=True)  45.9 us
    all_to_all x2, waiting for transfers between devices, spread(): return lax.all_to_all(copies, axis, split_axis=0, concat_axis=0, tiled=True)  31.8 us
    all_to_all x1, blocking collectives, on_device(): lax.all_to_all(back.reshape(experts, 2 * capacity, slice_width // 2), ('y...  27.7 us
    all_to_all x1, blocking collectives, on_device(): lax.all_to_all(send.reshape(experts, 2 * capacity, half), ('y', 'k'), spl...  24.5 us
    all_to_all x1, blocking collectives, on_device(): lax.all_to_all(partial_latent.reshape(nr, tok_rows, ny * unit), 'rep', sp...  24.5 us
    all_to_all x1, blocking collectives, spread(): return lax.all_to_all(copies, axis, split_axis=0, concat_axis=0, tiled=True)  22.3 us
    all_gather x1, waiting for transfers between devices, on_device(): full_rows = lax.all_gather(rows, 'rep', axis=0, tiled=True)  16.5 us
    all_to_all x2, starting transfers between devices, spread(): return lax.all_to_all(copies, axis, split_axis=0, concat_axis=0, tiled=True)  10.3 us
  transfers between devices with their start and end apart: 7, of which 5 were waited for; matrix products, arithmetic and copies ran while one was open for 4% of the time, Pallas kernels for 0%

profile of v6, /device:TPU:1, one launch (start us, length us, event | category | flops | bytes accessed | tf_op | source)
XLA Modules:
  0.0 253.2 jit_solution(920775703702002145)
XLA Ops:
  6.5 0.7 all-gather.5.cloned.1.call-update
  7.3 5.4 %collective-permute-start = (s32[4,128]{1,0:T(4,128)}, s32[4,128]{1,0:T(4,128)S(1)}, u32[]{:S(2)}, u32[]{:S(2)}) collective-permute-start(s32[4,128]{1,0:T(4,128)} %bitcast.94), channel_id=1, source_target_pairs={{0,0},{1,8},{2,16},{3,24},{4,32},{5,40},{6,48},{7,56},{8,1},{9,9},... | collective-permute-start | bytes 6152 | tf_op jit(solution)/shard_map/ppermute | solution.py:149
  12.7 1.7 broadcast_in_dim.87
  14.3 6.8 %all-to-all-start = ((bf16[8,32,1024]{2,1,0:T(8,128)(2,1)}), bf16[8,32,1024]{2,1,0:T(8,128)(2,1)S(1)}, u32[]{:S(2)}, u32[]{:S(2)}) async-start(bf16[8,32,1024]{2,1,0:T(8,128)(2,1)} %broadcast_in_dim.87), calls=%async_computation | async-start | bytes 1048576 | tf_op jit(solution)/shard_map/all_to_all | solution.py:13
  21.6 0.5 fusion.2
  22.1 17.0 %all-to-all-done = bf16[8,32,1024]{2,1,0:T(8,128)(2,1)S(1)} async-done(((bf16[8,32,1024]{2,1,0:T(8,128)(2,1)}), bf16[8,32,1024]{2,1,0:T(8,128)(2,1)S(1)}, u32[]{:S(2)}, u32[]{:S(2)}) %all-to-all-start) | async-done | bytes 524320 | tf_op jit(solution)/shard_map/all_to_all | solution.py:13
  39.1 6.8 %all-gather.5.cloned.1.call-done = bf16[1024,1024]{1,0:T(8,128)(2,1)} async-done(((bf16[128,1024]{1,0:T(8,128)(2,1)}), bf16[1024,1024]{1,0:T(8,128)(2,1)}) %all-gather.5.cloned.1.call-update) | async-done | bytes 2097168 | tf_op jit(solution)/shard_map/all_gather | solution.py:151
  46.0 2.3 convolution_convert_fusion.1
  48.3 24.5 %all_to_all.30 = bf16[8,128,256]{2,1,0:T(8,128)(2,1)S(1)} all-to-all(bf16[8,128,256]{2,1,0:T(8,128)(2,1)S(1)} %bitcast.91), channel_id=1, replica_groups=mesh['y'=8,'k'=8,'rep'=8] {'rep'}, dimensions={0} | all-to-all | bytes 1048576 | tf_op jit(solution)/shard_map/all_to_all | solution.py:163
  73.2 24.5 %all_to_all.31 = bf16[64,24,128]{2,1,0:T(8,128)(2,1)S(1)} all-to-all(bf16[64,24,128]{2,1,0:T(8,128)(2,1)S(1)} %bitcast.84), channel_id=1, replica_groups=mesh['y'=8,'k'=8,'rep'=8] {'y','k'}, dimensions={0} | all-to-all | bytes 786432 | tf_op jit(solution)/shard_map/all_to_all | solution.py:171
  97.8 0.8 copy.23
  99.5 0.8 broadcast_in_dim.103
  100.4 3.5 %all-to-all-start.3 = ((bf16[8,32,1024]{2,1,0:T(8,128)(2,1)}), bf16[8,32,1024]{2,1,0:T(8,128)(2,1)S(1)}, u32[]{:S(2)}, u32[]{:S(2)}) async-start(bf16[8,32,1024]{2,1,0:T(8,128)(2,1)} %broadcast_in_dim.103), calls=%async_computation.3 | async-start | bytes 1048576 | tf_op jit(solution)/shard_map/all_to_all | solution.py:13
  104.0 1.4 fusion
  105.5 1.5 pad_maximum_fusion.w_ref
  107.0 14.7 %all-to-all-done.3 = bf16[8,32,1024]{2,1,0:T(8,128)(2,1)S(1)} async-done(((bf16[8,32,1024]{2,1,0:T(8,128)(2,1)}), bf16[8,32,1024]{2,1,0:T(8,128)(2,1)S(1)}, u32[]{:S(2)}, u32[]{:S(2)}) %all-to-all-start.3) | async-done | bytes 524320 | tf_op jit(solution)/shard_map/all_to_all | solution.py:13
  121.8 16.5 %all-gather.7.cloned.1.call-done.x_ref = bf16[768,2048]{1,0:T(8,128)(2,1)} async-done(((bf16[96,2048]{1,0:T(8,128)(2,1)}), bf16[768,2048]{1,0:T(8,128)(2,1)}) %all-gather.7.cloned.1.call-update) | async-done | bytes 3145744 | tf_op jit(solution)/shard_map/all_gather | solution.py:178
  138.3 6.4 %shard_map.82 = bf16[768,2048]{1,0:T(8,128)(2,1)} custom-call(bf16[768,2048]{1,0:T(8,128)(2,1)} %all-gather.7.cloned.1.call-done.x_ref, bf16[2048,512]{1,0:T(8,128)(2,1)} %pad_maximum_fusion.w_ref, bf16[256,2048]{1,0:T(8,128)(2,1)} %bitcast.87), custom_call_target="tpu_custom_call" | custom-call | flops 2415919104 | bytes 9437184 | tf_op jit(solution)/shard_map/pallas_call | solution.py:48
  144.8 45.9 %reduce-scatter.2.cloned.1.call-done = bf16[768,256]{1,0:T(8,128)(2,1)} async-done(((bf16[768,2048]{1,0:T(8,128)(2,1)}), bf16[768,256]{1,0:T(8,128)(2,1)}) %reduce-scatter.2.cloned.1.call-update) | async-done | bytes 393232 | tf_op jit(solution)/shard_map/reduce_scatter | solution.py:190
  190.7 1.3 copy.26
  192.2 27.7 %all_to_all.32 = bf16[64,24,128]{2,1,0:T(8,128)(2,1)S(1)} all-to-all(bf16[64,24,128]{2,1,0:T(8,128)(2,1)S(1)} %copy.27), channel_id=1, replica_groups=mesh['y'=8,'k'=8,'rep'=8] {'y','k'}, dimensions={0} | all-to-all | bytes 786432 | tf_op jit(solution)/shard_map/all_to_all | solution.py:194
  220.3 0.4 fusion.3
  220.8 22.3 %all_to_all.33.x_ref = bf16[8,256,128]{2,1,0:T(8,128)(2,1)} all-to-all(bf16[8,256,128]{2,1,0:T(8,128)(2,1)S(1)} %broadcast_in_dim.104), channel_id=1, replica_groups=mesh['y'=8,'k'=8,'rep'=8] {'rep'}, dimensions={0} | all-to-all | bytes 1048576 | tf_op jit(solution)/shard_map/all_to_all | solution.py:13
  243.1 3.6 %shard_map.83 = bf16[128,1024]{1,0:T(8,128)(2,1)} custom-call(bf16[8,256,128]{2,1,0:T(8,128)(2,1)} %all_to_all.33.x_ref, bf16[8,8,32,1024]{3,2,1,0:T(8,128)(2,1)} %bitcast.78), custom_call_target="tpu_custom_call" | custom-call | flops 536870912 | bytes 4194304 | tf_op jit(solution)/shard_map/pallas_call | solution.py:88
  (48 shorter events, 2.7 us)
Async XLA Ops:
  6.5 39.4 %all-gather.5.cloned.1.call-start = ((), (), s32[]{:S(2)}) async-start(), calls=%async_computation.7 | async-start | bytes 2359296 | tf_op jit(solution)/shard_map/all_gather | solution.py:151
  7.3 14.2 %collective-permute-start = (s32[4,128]{1,0:T(4,128)}, s32[4,128]{1,0:T(4,128)S(1)}, u32[]{:S(2)}, u32[]{:S(2)}) collective-permute-start(s32[4,128]{1,0:T(4,128)} %bitcast.94), channel_id=1, source_target_pairs={{0,0},{1,8},{2,16},{3,24},{4,32},{5,40},{6,48},{7,56},{8,1},{9,9},... | collective-permute-start | bytes 6152 | tf_op jit(solution)/shard_map/ppermute | solution.py:149
  14.3 24.8 %all-to-all-start = ((bf16[8,32,1024]{2,1,0:T(8,128)(2,1)}), bf16[8,32,1024]{2,1,0:T(8,128)(2,1)S(1)}, u32[]{:S(2)}, u32[]{:S(2)}) async-start(bf16[8,32,1024]{2,1,0:T(8,128)(2,1)} %broadcast_in_dim.87), calls=%async_computation | async-start | bytes 1048576 | tf_op jit(solution)/shard_map/all_to_all | solution.py:13
  21.2 117.1 %all-gather.7.cloned.1.call-start = ((), (), s32[]{:S(2)}) async-start(), calls=%async_computation.8 | async-start | bytes 3538944 | tf_op jit(solution)/shard_map/all_gather | solution.py:178
  72.8 25.8 %copy-start.2 = (bf16[1,2048,256]{2,1,0:T(8,128)(2,1)S(1)}, bf16[1,2048,256]{2,1,0:T(8,128)(2,1)}, u32[]{:S(2)}) copy-start(bf16[1,2048,256]{2,1,0:T(8,128)(2,1)} %param.10) | copy-start | bytes 3145732
  97.7 1.4 copy-start.3
  98.6 0.8 copy-start.5
  98.6 0.9 copy-start.4
  98.7 5.2 %copy-start.6 = (f32[128,4]{0,1:T(4,128)S(1)}, f32[128,4]{0,1:T(4,128)}, u32[]{:S(2)}) copy-start(f32[128,4]{0,1:T(4,128)} %param.15) | copy-start | bytes 6148
  100.4 21.4 %all-to-all-start.3 = ((bf16[8,32,1024]{2,1,0:T(8,128)(2,1)}), bf16[8,32,1024]{2,1,0:T(8,128)(2,1)S(1)}, u32[]{:S(2)}, u32[]{:S(2)}) async-start(bf16[8,32,1024]{2,1,0:T(8,128)(2,1)} %broadcast_in_dim.103), calls=%async_computation.3 | async-start | bytes 1048576 | tf_op jit(solution)/shard_map/all_to_all | solution.py:13
  103.9 86.8 %reduce-scatter.2.cloned.1.call-start = ((), (), s32[]{:S(2)}) async-start(), calls=%async_computation.9 | async-start | bytes 3538944 | tf_op jit(solution)/shard_map/reduce_scatter | solution.py:190
  121.8 22.9 %copy-start.1 = (bf16[8,32,1024]{2,1,0:T(8,128)(2,1)}, bf16[8,32,1024]{2,1,0:T(8,128)(2,1)S(1)}, u32[]{:S(2)}) copy-start(bf16[8,32,1024]{2,1,0:T(8,128)(2,1)S(1)} %all-to-all-done.3) | copy-start | bytes 1572868
  144.7 75.6 %copy-start = (bf16[1536,256]{1,0:T(8,128)(2,1)S(1)}, bf16[1536,256]{1,0:T(8,128)(2,1)}, u32[]{:S(2)}) copy-start(bf16[1536,256]{1,0:T(8,128)(2,1)} %get-tuple-element.25) | copy-start | bytes 2359300
  144.7 98.3 %all-gather.9.cloned.1.call-start = ((), (), s32[]{:S(2)}) async-start(), calls=%async_computation.10 | async-start | bytes 4718592 | tf_op jit(solution)/shard_map/all_gather | solution.py:192
Sparse Core Ops, SparseCore 0:
  9.5 36.4 all-gather.4
  98.7 39.4 all-gather.6
  144.9 45.7 reduce-scatter.1
  192.7 41.5 all-gather.8

commit v7 on v6

--- a/solution.py
+++ b/solution.py
@@ -145,11 +145,13 @@
     slice_width = width // nr
 
     swap = [(i * nr + j, j * nr + i) for i in range(nk) for j in range(nr)]
+    copies = jnp.broadcast_to(down_weight.T[None], (ny, unit, down_weight.shape[0]))
     ids_t = expert_ids.T
-    sent_ids_t = lax.ppermute(ids_t, ("k", "rep"), swap)
+    after, copies = lax.optimization_barrier((ids_t, copies))
+    sent_ids_t = lax.ppermute(after, ("k", "rep"), swap)
 
     all_tokens = lax.all_gather(tokens, "k", axis=0, tiled=True)
-    down_cols = spread(down_weight.T, "y").reshape(ny * unit, down_weight.shape[0])
+    down_cols = lax.all_to_all(copies, "y", split_axis=0, concat_axis=0, tiled=True).reshape(ny * unit, down_weight.shape[0])
     one_hot, counts = expert_counts(sent_ids_t, experts)
     select = slot_mask(one_hot, counts, capacity).astype(jnp.bfloat16)
     select = select.reshape(2 * experts * capacity, 2 * tok_rows)

time: 254 us -> 254 us (level)
    all_to_all x2 -> x1, waiting for transfers between devices: 31.8 us -> 14.7 us  [spread(): return lax.all_to_all(copies, axis, split_axis=0, concat_axis=0, tiled=True)]
    all_gather x1, waiting for transfers between devices: 6.83 us -> 14.6 us  [on_device(): all_tokens = lax.all_gather(tokens, 'k', axis=0, tiled=True)]
    all_to_all x0 -> x1, starting transfers between devices: none -> 7.65 us  [on_device(): lax.all_to_all(copies, 'y', split_axis=0, concat_axis=0, tiled=True)]
    all_to_all x0 -> x1, waiting for transfers between devices: none -> 7.46 us  [on_device(): lax.all_to_all(copies, 'y', split_axis=0, concat_axis=0, tiled=True)]
    all_to_all x2 -> x1, starting transfers between devices: 10.3 us -> 3.49 us  [spread(): return lax.all_to_all(copies, axis, split_axis=0, concat_axis=0, tiled=True)]
  transfers between devices with their start and end apart: 7 -> 7, of which waited for: 5 -> 6; matrix products, arithmetic and copies ran while one was open for 4% -> 4% of each run, Pallas kernels for 0% -> 0%
where the time goes in v7:
time: 254 us; the launch traced here: 253 us
  waiting for transfers between devices  101 us (40%)
  blocking collectives  99 us (39%)
  starting transfers between devices  16.1 us (6%)
  between operations  13.4 us (5%)
  Pallas kernels  10 us (4%)
  local copies, waits for them, and re-layouts  6.05 us (2%)
  matrix products  3.8 us (1%)
  other arithmetic  3.61 us (1%)
    reduce_scatter x1, waiting for transfers between devices, on_device(): lax.psum_scatter(partial_out, 'rep', scatter_dimension=1, tiled=True)  45.8 us
    all_to_all x1, blocking collectives, on_device(): lax.all_to_all(back.reshape(experts, 2 * capacity, slice_width // 2), ('y...  27.9 us
    all_to_all x1, blocking collectives, on_device(): lax.all_to_all(send.reshape(experts, 2 * capacity, half), ('y', 'k'), spl...  24.6 us
    all_to_all x1, blocking collectives, on_device(): lax.all_to_all(partial_latent.reshape(nr, tok_rows, ny * unit), 'rep', sp...  24.4 us
    all_to_all x1, blocking collectives, spread(): return lax.all_to_all(copies, axis, split_axis=0, concat_axis=0, tiled=True)  22.2 us
    all_gather x1, waiting for transfers between devices, on_device(): full_rows = lax.all_gather(rows, 'rep', axis=0, tiled=True)  16.5 us
    all_to_all x1, waiting for transfers between devices, spread(): return lax.all_to_all(copies, axis, split_axis=0, concat_axis=0, tiled=True)  14.7 us
    all_gather x1, waiting for transfers between devices, on_device(): all_tokens = lax.all_gather(tokens, 'k', axis=0, tiled=True)  14.6 us
  transfers between devices with their start and end apart: 7, of which 6 were waited for; matrix products, arithmetic and copies ran while one was open for 4% of the time, Pallas kernels for 0%

profile of v7, /device:TPU:1, one launch (start us, length us, event | category | flops | bytes accessed | tf_op | source)
XLA Modules:
  0.0 253.3 jit_solution(1725690497009921467)
XLA Ops:
  6.5 0.7 all-gather.5.cloned.1.call-update
  7.3 1.7 broadcast_in_dim.87
  8.9 7.7 %all-to-all-start = ((bf16[8,32,1024]{2,1,0:T(8,128)(2,1)}), bf16[8,32,1024]{2,1,0:T(8,128)(2,1)S(1)}, u32[]{:S(2)}, u32[]{:S(2)}) async-start(bf16[8,32,1024]{2,1,0:T(8,128)(2,1)} %broadcast_in_dim.87), calls=%async_computation | async-start | bytes 1048576 | tf_op jit(solution)/shard_map/all_to_all | solution.py:154
  16.6 4.8 %collective-permute-start = (s32[4,128]{1,0:T(4,128)}, s32[4,128]{1,0:T(4,128)S(1)}, u32[]{:S(2)}, u32[]{:S(2)}) collective-permute-start(s32[4,128]{1,0:T(4,128)} %bitcast.99), channel_id=1, source_target_pairs={{0,0},{1,8},{2,16},{3,24},{4,32},{5,40},{6,48},{7,56},{8,1},{9,9},... | collective-permute-start | bytes 6152 | tf_op jit(solution)/shard_map/ppermute | solution.py:151
  21.7 1.5 collective-permute-done
  23.4 0.5 fusion.2
  23.9 7.5 %all-to-all-done = bf16[8,32,1024]{2,1,0:T(8,128)(2,1)S(1)} async-done(((bf16[8,32,1024]{2,1,0:T(8,128)(2,1)}), bf16[8,32,1024]{2,1,0:T(8,128)(2,1)S(1)}, u32[]{:S(2)}, u32[]{:S(2)}) %all-to-all-start) | async-done | bytes 524320 | tf_op jit(solution)/shard_map/all_to_all | solution.py:154
  31.4 14.6 %all-gather.5.cloned.1.call-done = bf16[1024,1024]{1,0:T(8,128)(2,1)} async-done(((bf16[128,1024]{1,0:T(8,128)(2,1)}), bf16[1024,1024]{1,0:T(8,128)(2,1)}) %all-gather.5.cloned.1.call-update) | async-done | bytes 2097168 | tf_op jit(solution)/shard_map/all_gather | solution.py:153
  45.9 2.3 fusion.3
  48.4 24.4 %all_to_all.30 = bf16[8,128,256]{1,2,0:T(8,128)(2,1)S(1)} all-to-all(bf16[8,128,256]{1,2,0:T(8,128)(2,1)S(1)} %copy_bitcast_fusion), channel_id=1, replica_groups=mesh['y'=8,'k'=8,'rep'=8] {'rep'}, dimensions={0} | all-to-all | bytes 1048576 | tf_op jit(solution)/shard_map/all_to_all | solution.py:165
  73.2 24.6 %all_to_all.31 = bf16[64,24,128]{2,1,0:T(8,128)(2,1)S(1)} all-to-all(bf16[64,24,128]{2,1,0:T(8,128)(2,1)S(1)} %bitcast.90), channel_id=1, replica_groups=mesh['y'=8,'k'=8,'rep'=8] {'y','k'}, dimensions={0} | all-to-all | bytes 786432 | tf_op jit(solution)/shard_map/all_to_all | solution.py:173
  97.9 0.8 copy.25
  99.6 0.8 broadcast_in_dim.103
  100.5 3.5 %all-to-all-start.3 = ((bf16[8,32,1024]{2,1,0:T(8,128)(2,1)}), bf16[8,32,1024]{2,1,0:T(8,128)(2,1)S(1)}, u32[]{:S(2)}, u32[]{:S(2)}) async-start(bf16[8,32,1024]{2,1,0:T(8,128)(2,1)} %broadcast_in_dim.103), calls=%async_computation.3 | async-start | bytes 1048576 | tf_op jit(solution)/shard_map/all_to_all | solution.py:13
  104.1 1.4 fusion
  105.6 1.5 pad_maximum_fusion.w_ref
  107.1 14.7 %all-to-all-done.3 = bf16[8,32,1024]{2,1,0:T(8,128)(2,1)S(1)} async-done(((bf16[8,32,1024]{2,1,0:T(8,128)(2,1)}), bf16[8,32,1024]{2,1,0:T(8,128)(2,1)S(1)}, u32[]{:S(2)}, u32[]{:S(2)}) %all-to-all-start.3) | async-done | bytes 524320 | tf_op jit(solution)/shard_map/all_to_all | solution.py:13
  121.9 16.5 %all-gather.7.cloned.1.call-done.x_ref = bf16[768,2048]{1,0:T(8,128)(2,1)} async-done(((bf16[96,2048]{1,0:T(8,128)(2,1)}), bf16[768,2048]{1,0:T(8,128)(2,1)}) %all-gather.7.cloned.1.call-update) | async-done | bytes 3145744 | tf_op jit(solution)/shard_map/all_gather | solution.py:180
  138.4 6.4 %shard_map.82 = bf16[768,2048]{1,0:T(8,128)(2,1)} custom-call(bf16[768,2048]{1,0:T(8,128)(2,1)} %all-gather.7.cloned.1.call-done.x_ref, bf16[2048,512]{1,0:T(8,128)(2,1)} %pad_maximum_fusion.w_ref, bf16[256,2048]{1,0:T(8,128)(2,1)} %bitcast.93), custom_call_target="tpu_custom_call" | custom-call | flops 2415919104 | bytes 9437184 | tf_op jit(solution)/shard_map/pallas_call | solution.py:48
  144.9 45.8 %reduce-scatter.2.cloned.1.call-done = bf16[768,256]{1,0:T(8,128)(2,1)} async-done(((bf16[768,2048]{1,0:T(8,128)(2,1)}), bf16[768,256]{1,0:T(8,128)(2,1)}) %reduce-scatter.2.cloned.1.call-update) | async-done | bytes 393232 | tf_op jit(solution)/shard_map/reduce_scatter | solution.py:192
  190.7 1.3 copy.28
  192.2 27.9 %all_to_all.32 = bf16[64,24,128]{2,1,0:T(8,128)(2,1)S(1)} all-to-all(bf16[64,24,128]{2,1,0:T(8,128)(2,1)S(1)} %copy.29), channel_id=1, replica_groups=mesh['y'=8,'k'=8,'rep'=8] {'y','k'}, dimensions={0} | all-to-all | bytes 786432 | tf_op jit(solution)/shard_map/all_to_all | solution.py:196
  221.0 22.2 %all_to_all.33.x_ref = bf16[8,256,128]{2,1,0:T(8,128)(2,1)} all-to-all(bf16[8,256,128]{2,1,0:T(8,128)(2,1)S(1)} %broadcast_in_dim.104), channel_id=1, replica_groups=mesh['y'=8,'k'=8,'rep'=8] {'rep'}, dimensions={0} | all-to-all | bytes 1048576 | tf_op jit(solution)/shard_map/all_to_all | solution.py:13
  243.2 3.6 %shard_map.83 = bf16[128,1024]{1,0:T(8,128)(2,1)} custom-call(bf16[8,256,128]{2,1,0:T(8,128)(2,1)} %all_to_all.33.x_ref, bf16[8,8,32,1024]{3,2,1,0:T(8,128)(2,1)} %bitcast.84), custom_call_target="tpu_custom_call" | custom-call | flops 536870912 | bytes 4194304 | tf_op jit(solution)/shard_map/pallas_call | solution.py:88
  (49 shorter events, 3.2 us)
Async XLA Ops:
  6.5 39.4 %all-gather.5.cloned.1.call-start = ((), (), s32[]{:S(2)}) async-start(), calls=%async_computation.7 | async-start | bytes 2359296 | tf_op jit(solution)/shard_map/all_gather | solution.py:153
  8.9 22.4 %all-to-all-start = ((bf16[8,32,1024]{2,1,0:T(8,128)(2,1)}), bf16[8,32,1024]{2,1,0:T(8,128)(2,1)S(1)}, u32[]{:S(2)}, u32[]{:S(2)}) async-start(bf16[8,32,1024]{2,1,0:T(8,128)(2,1)} %broadcast_in_dim.87), calls=%async_computation | async-start | bytes 1048576 | tf_op jit(solution)/shard_map/all_to_all | solution.py:154
  16.6 121.8 %all-gather.7.cloned.1.call-start = ((), (), s32[]{:S(2)}) async-start(), calls=%async_computation.8 | async-start | bytes 3538944 | tf_op jit(solution)/shard_map/all_gather | solution.py:180
  16.6 6.6 %collective-permute-start = (s32[4,128]{1,0:T(4,128)}, s32[4,128]{1,0:T(4,128)S(1)}, u32[]{:S(2)}, u32[]{:S(2)}) collective-permute-start(s32[4,128]{1,0:T(4,128)} %bitcast.99), channel_id=1, source_target_pairs={{0,0},{1,8},{2,16},{3,24},{4,32},{5,40},{6,48},{7,56},{8,1},{9,9},... | collective-permute-start | bytes 6152 | tf_op jit(solution)/shard_map/ppermute | solution.py:151
  72.8 25.9 %copy-start.2 = (bf16[1,2048,256]{2,1,0:T(8,128)(2,1)S(1)}, bf16[1,2048,256]{2,1,0:T(8,128)(2,1)}, u32[]{:S(2)}) copy-start(bf16[1,2048,256]{2,1,0:T(8,128)(2,1)} %param.10) | copy-start | bytes 3145732
  97.8 1.4 copy-start.3
  98.7 0.8 copy-start.5
  98.7 0.9 copy-start.4
  98.8 5.2 %copy-start.6 = (f32[128,4]{0,1:T(4,128)S(1)}, f32[128,4]{0,1:T(4,128)}, u32[]{:S(2)}) copy-start(f32[128,4]{0,1:T(4,128)} %param.15) | copy-start | bytes 6148
  100.5 21.4 %all-to-all-start.3 = ((bf16[8,32,1024]{2,1,0:T(8,128)(2,1)}), bf16[8,32,1024]{2,1,0:T(8,128)(2,1)S(1)}, u32[]{:S(2)}, u32[]{:S(2)}) async-start(bf16[8,32,1024]{2,1,0:T(8,128)(2,1)} %broadcast_in_dim.103), calls=%async_computation.3 | async-start | bytes 1048576 | tf_op jit(solution)/shard_map/all_to_all | solution.py:13
  104.0 86.7 %reduce-scatter.2.cloned.1.call-start = ((), (), s32[]{:S(2)}) async-start(), calls=%async_computation.9 | async-start | bytes 3538944 | tf_op jit(solution)/shard_map/reduce_scatter | solution.py:192
  121.9 22.9 %copy-start.1 = (bf16[8,32,1024]{2,1,0:T(8,128)(2,1)}, bf16[8,32,1024]{2,1,0:T(8,128)(2,1)S(1)}, u32[]{:S(2)}) copy-start(bf16[8,32,1024]{2,1,0:T(8,128)(2,1)S(1)} %all-to-all-done.3) | copy-start | bytes 1572868
  144.8 75.7 %copy-start = (bf16[1536,256]{1,0:T(8,128)(2,1)S(1)}, bf16[1536,256]{1,0:T(8,128)(2,1)}, u32[]{:S(2)}) copy-start(bf16[1536,256]{1,0:T(8,128)(2,1)} %get-tuple-element.29) | copy-start | bytes 2359300
  144.8 98.3 %all-gather.9.cloned.1.call-start = ((), (), s32[]{:S(2)}) async-start(), calls=%async_computation.10 | async-start | bytes 4718592 | tf_op jit(solution)/shard_map/all_gather | solution.py:194
Sparse Core Ops, SparseCore 0:
  9.5 36.3 all-gather.4
  98.8 39.5 all-gather.6
  144.9 45.6 reduce-scatter.1
  192.7 41.7 all-gather.8
